TPU v7x, 512 devices: a whole 4x8x8 slice. The times are simulated.
512 devices in a mesh: expert: 128 (over z, y, core), pair: 4 (over x).
Axes of the slice: x: 4, y: 8, z: 8, core: 2. Of those that a mesh axis runs over, the one named last changes fastest.
Arguments:
- tokens: bfloat16 [2048, 4096], P('expert', 'pair'), may hold values from -6 to 6
- routes: int32 [2048, 8], P('expert'), may hold values from 0 to 127, as said below
- router_probs: float32 [2048, 8], P('expert'), may hold values from 0.02 to 1
- w_gate: bfloat16 [128, 768, 4096], P('expert', 'pair'), may hold values from -0.09375 to 0.09375
- w_up: bfloat16 [128, 768, 4096], P('expert', 'pair'), may hold values from -0.09375 to 0.09375
- w_down: bfloat16 [128, 768, 4096], P('expert', 'pair'), may hold values from -0.4375 to 0.4375
Outputs:
- expert_mix: bfloat16 [2048, 4096], P('expert', 'pair')
Inputs may be any that keep to these rules, and one draw needn't show every extreme that they name: `routes`: each row names 8 different experts. In every aligned block of 16 rows (one index of expert's micro-batch; micro-batch m of that index is its rows m * 16 to (m + 1) * 16 - 1), exactly half of the 128 experts are named, each by exactly 2 rows.
All inputs are finite; a program needn't handle non-finite values.
Results may differ from a plain program's by a relative error of at most 0.017.
Values may be sent and summed in bfloat16 or wider, within the bound.
A program may use at most 64 MiB of HBM per device.

v0:
```python
import jax
import jax.numpy as jnp
from jax import lax
from jax.sharding import PartitionSpec as P

TOP = 8
TOK_MB = 16


def slot_ranks(flat_routes):
    same_expert = flat_routes[..., :, None] == flat_routes[..., None, :]
    count = flat_routes.shape[-1]
    earlier = jnp.arange(count)[:, None] > jnp.arange(count)[None, :]
    return jnp.sum(jnp.logical_and(same_expert, earlier), axis=-1)


def combine_rows(returned, target, mixing, micro_count, width_slots):
    picked = jnp.take_along_axis(
        returned.reshape(micro_count, width_slots, -1), target[:, :, None], axis=1
    )
    picked = picked.reshape(micro_count, TOK_MB, TOP, -1).astype(jnp.float32)
    return jnp.einsum("mtk,mtkd->mtd", mixing, picked)


def per_device(tokens, routes, router_probs, w_gate, w_up, w_down):
    tok_rows = tokens.shape[0]
    micro_count = tok_rows // TOK_MB
    expert_count = lax.axis_size("expert")
    local_count = w_gate.shape[0]
    experts_all = expert_count * local_count
    capacity = 2 * TOK_MB * TOP // experts_all
    width_slots = experts_all * capacity
    flat_routes = routes.reshape(micro_count, TOK_MB * TOP)
    target = flat_routes * capacity + slot_ranks(flat_routes)
    slot_hits = target[:, None, :] == jnp.arange(width_slots, dtype=jnp.int32)[None, :, None]
    placing = jnp.any(slot_hits.reshape(micro_count, width_slots, TOK_MB, TOP), axis=-1).astype(
        jnp.bfloat16
    )
    gathered = lax.all_gather(tokens, "pair", axis=1, tiled=True)
    outgoing = jnp.einsum(
        "mst,mtd->msd",
        placing,
        gathered.reshape(micro_count, TOK_MB, -1),
        preferred_element_type=jnp.float32,
    ).astype(jnp.bfloat16)
    outgoing = outgoing.reshape(micro_count, expert_count, local_count * capacity, -1)
    arrived = lax.all_to_all(outgoing, "expert", split_axis=1, concat_axis=1, tiled=True)
    slot_rows = arrived.reshape(micro_count, expert_count, local_count, capacity, -1)
    gate_act = jnp.einsum("mslcd,lfd->mslcf", slot_rows, w_gate, preferred_element_type=jnp.float32)
    up_act = jnp.einsum("mslcd,lfd->mslcf", slot_rows, w_up, preferred_element_type=jnp.float32)
    hidden = (jax.nn.silu(gate_act) * up_act).astype(jnp.bfloat16)
    down_act = jnp.einsum("mslcf,lfd->mslcd", hidden, w_down, preferred_element_type=jnp.float32)
    partial_value = down_act.astype(jnp.bfloat16)
    mixing = router_probs / jnp.sum(router_probs, axis=-1, keepdims=True)
    mixing = mixing.reshape(micro_count, TOK_MB, TOP)
    outbound = partial_value.reshape(micro_count, expert_count, local_count * capacity, -1)
    returned = lax.all_to_all(outbound, "expert", split_axis=1, concat_axis=1, tiled=True)
    mixture = combine_rows(returned, target, mixing, micro_count, width_slots)
    own_share = lax.psum_scatter(
        mixture.reshape(tok_rows, -1).astype(jnp.bfloat16), "pair", scatter_dimension=1, tiled=True
    )
    return own_share


def solution(mesh):
    in_specs = (
        P("expert", "pair"),
        P("expert", None),
        P("expert", None),
        P("expert", "pair", None),
        P("expert", "pair", None),
        P("expert", "pair", None),
    )
    out_specs = P("expert", "pair")
    return jax.shard_map(
        per_device, mesh=mesh, in_specs=in_specs, out_specs=out_specs, check_vma=False
    )
```

profile of v0, /device:TPU:1, one launch (start us, length us, event | category | flops | bytes accessed | tf_op | source)
XLA Modules:
  0.0 208.2 jit_solution(6384301346555285970)
XLA Ops:
  6.5 0.9 copy.19
  7.4 0.1 eq.45
  7.5 0.2 convert_reduce_fusion
  7.7 0.1 reduce_sum.24
  7.8 0.1 fusion.47
  7.9 10.5 %all_gather.3 = bf16[16,4096]{1,0:T(8,128)(2,1)S(1)} all-gather(bf16[16,1024]{1,0:T(8,128)(2,1)} %param.6), channel_id=1, replica_groups=mesh['expert'=128,'pair'=4] {'pair'}, dimensions={1}, use_global_device_ids=true | all-gather | bytes 163840 | tf_op jit(solution)/shard_map/all_gather | solution.py:39
  18.4 2.1 %convolution_convert_fusion.1 = bf16[256,4096]{1,0:T(8,128)(2,1)} fusion(pred[256,16]{0,1:T(8,128)(4,1)S(1)} %fusion.47, bf16[16,4096]{1,0:T(8,128)(2,1)S(1)} %all_gather.3), kind=kOutput, calls=%fused_computation.2 | convolution fusion | flops 34603008 | bytes 2232320 | tf_op jit(solution)/shard_map/mst,mtd->msd/dot_general | solution.py:40
  20.5 4.4 %reshape.293 = bf16[1,128,2,4096]{3,2,1,0:T(2,128)(2,1)} reshape(bf16[256,4096]{1,0:T(8,128)(2,1)} %convolution_convert_fusion.1) | data formatting | bytes 4194304 | tf_op jit(solution)/shard_map/reshape | solution.py:46
  24.9 71.9 %all_to_all.10 = bf16[1,128,2,4096]{3,2,0,1:T(2,128)(2,1)S(1)} all-to-all(bf16[1,128,2,4096]{3,2,0,1:T(2,128)(2,1)} %bitcast.93), channel_id=1, replica_groups=mesh['expert'=128,'pair'=4] {'expert'}, dimensions={1} | all-to-all | bytes 4194304 | tf_op jit(solution)/shard_map/all_to_all | solution.py:47
  96.8 1.3 copy-done.1
  98.1 2.5 %fusion.10 = f32[1,128,1,2,192]{1,4,3,0,2:T(8,128)S(1)} fusion(bf16[1,192,4096]{2,1,0:T(8,128)(2,1)S(1)} %copy-done.4, bf16[1,128,2,4096]{3,2,0,1:T(2,128)(2,1)S(1)} %all_to_all.10), kind=kOutput, calls=%fused_computation.13 | convolution fusion | flops 402653184 | bytes 3866624 | tf_op jit(solution)/shard_map/mslcd,lfd->mslcf/dot_general | solution.py:49
  100.6 6.7 %fusion = bf16[1,128,2,4096]{3,1,2,0:T(8,128)(2,1)} fusion(bf16[1,192,4096]{2,1,0:T(8,128)(2,1)S(1)} %copy-done, bf16[1,192,4096]{2,1,0:T(8,128)(2,1)S(1)} %copy-done.2, bf16[1,128,2,4096]{3,2,0,1:T(2,128)(2,1)} %copy-done.1, f32[1,128,1,2,192]{1,4,3,0,2:T(8,128)S(1)} %fusion.10), kind=kOutput, calls=%fused_computation.3 | convolution fusion | flops 806649856 | bytes 7536640 | tf_op jit(solution)/shard_map/mslcf,lfd->mslcd/dot_general | solution.py:52
  107.4 5.1 %copy.23 = bf16[1,128,2,4096]{3,2,0,1:T(2,128)(2,1)} copy(bf16[1,128,2,4096]{3,1,2,0:T(8,128)(2,1)} %fusion) | data formatting | bytes 4194304 | tf_op jit(solution)/shard_map/reshape | solution.py:56
  112.4 9.5 %all-to-all-start.1 = ((bf16[1,128,2,4096]{3,2,0,1:T(2,128)(2,1)}), bf16[1,128,2,4096]{3,2,0,1:T(2,128)(2,1)}, u32[]{:S(2)}, u32[]{:S(2)}) async-start(bf16[1,128,2,4096]{3,2,0,1:T(2,128)(2,1)} %copy.23), calls=%async_computation.1 | async-start | bytes 4194304 | tf_op jit(solution)/shard_map/all_to_all | solution.py:57
  122.0 0.3 reduce-scatter.2.cloned.1.call-start
  122.3 0.1 mul.60
  122.4 0.1 copy.24
  122.5 50.4 %all-to-all-done.1 = bf16[1,128,2,4096]{3,2,0,1:T(2,128)(2,1)} async-done(((bf16[1,128,2,4096]{3,2,0,1:T(2,128)(2,1)}), bf16[1,128,2,4096]{3,2,0,1:T(2,128)(2,1)}, u32[]{:S(2)}, u32[]{:S(2)}) %all-to-all-start.1) | async-done | bytes 2097184 | tf_op jit(solution)/shard_map/all_to_all | solution.py:57
  172.9 4.1 %reshape.301 = bf16[256,4096]{1,0:T(8,128)(2,1)} reshape(bf16[1,128,2,4096]{3,2,0,1:T(2,128)(2,1)} %all-to-all-done.1) | data formatting | bytes 4194304 | tf_op jit(solution)/shard_map/reshape | solution.py:19
  177.0 4.1 %gather_fusion = bf16[128,4096]{1,0:T(8,128)(2,1)S(1)} fusion(bf16[256,4096]{1,0:T(8,128)(2,1)} %reshape.301, s32[1024]{0:T(1024)S(1)} %pad_clamp_fusion), kind=kCustom, calls=%fused_computation | custom fusion | bytes 2097664 | tf_op jit(solution)/shard_map/jit(take_along_axis)/gather | solution.py:18
  181.1 0.5 fusion.35
  181.6 0.8 copy.47
  182.4 0.0 reduce-scatter.2.cloned.1.call-update
  182.4 18.9 %reduce-scatter.2.cloned.1.call-done = bf16[16,1024]{1,0:T(8,128)(2,1)} async-done(((bf16[16,4096]{1,0:T(8,128)(2,1)}), bf16[16,1024]{1,0:T(8,128)(2,1)}) %reduce-scatter.2.cloned.1.call-update) | async-done | bytes 32784 | tf_op jit(solution)/shard_map/reduce_scatter | solution.py:59
  (15 shorter events, 0.1 us)
Async XLA Ops:
  6.5 94.1 %copy-start = (bf16[1,192,4096]{2,1,0:T(8,128)(2,1)S(1)}, bf16[1,192,4096]{2,1,0:T(8,128)(2,1)}, u32[]{:S(2)}) copy-start(bf16[1,192,4096]{2,1,0:T(8,128)(2,1)} %param.11) | copy-start | bytes 4718596
  24.9 73.2 %copy-start.4 = (bf16[1,192,4096]{2,1,0:T(8,128)(2,1)S(1)}, bf16[1,192,4096]{2,1,0:T(8,128)(2,1)}, u32[]{:S(2)}) copy-start(bf16[1,192,4096]{2,1,0:T(8,128)(2,1)} %param.9) | copy-start | bytes 4718596
  96.8 1.3 copy-start.1
  98.1 2.5 %copy-start.2 = (bf16[1,192,4096]{2,1,0:T(8,128)(2,1)S(1)}, bf16[1,192,4096]{2,1,0:T(8,128)(2,1)}, u32[]{:S(2)}) copy-start(bf16[1,192,4096]{2,1,0:T(8,128)(2,1)} %param.10) | copy-start | bytes 4718596
  112.4 9.9 %copy-start.3 = (f32[16,8]{0,1:T(8,128)S(1)}, f32[16,8]{0,1:T(8,128)}, u32[]{:S(2)}) copy-start(f32[16,8]{0,1:T(8,128)} %param.8) | copy-start | bytes 1540
  112.4 60.5 %all-to-all-start.1 = ((bf16[1,128,2,4096]{3,2,0,1:T(2,128)(2,1)}), bf16[1,128,2,4096]{3,2,0,1:T(2,128)(2,1)}, u32[]{:S(2)}, u32[]{:S(2)}) async-start(bf16[1,128,2,4096]{3,2,0,1:T(2,128)(2,1)} %copy.23), calls=%async_computation.1 | async-start | bytes 4194304 | tf_op jit(solution)/shard_map/all_to_all | solution.py:57
  122.0 79.3 %reduce-scatter.2.cloned.1.call-start = ((), (), s32[]{:S(2)}) async-start(), calls=%async_computation.3 | async-start | bytes 163840 | tf_op jit(solution)/shard_map/reduce_scatter | solution.py:59
Sparse Core Ops, SparseCore 0:
  182.5 18.7 reduce-scatter.1
where the time goes:
time: 210 us; the launch traced here: 208 us
  blocking collectives  82.4 us (39%)
  waiting for transfers between devices  69.3 us (33%)
  local copies, waits for them, and re-layouts  21 us (10%)
  between operations  13.5 us (6%)
  matrix products  11.8 us (6%)
  starting transfers between devices  9.79 us (5%)
    all_to_all x1, blocking collectives, per_device(): lax.all_to_all(outgoing, 'expert', split_axis=1, concat_axis=1, tiled=True)  71.9 us
    all_to_all x1, waiting for transfers between devices, per_device(): lax.all_to_all(outbound, 'expert', split_axis=1, concat_axis=1, tiled=True)  50.4 us
    reduce_scatter x1, waiting for transfers between devices, per_device(): lax.psum_scatter(mixture.reshape(tok_rows, -1).astype(jnp.bfloat16), 'pai...  18.9 us
    all_gather x1, blocking collectives, per_device(): gathered = lax.all_gather(tokens, 'pair', axis=1, tiled=True)  10.5 us
    all_to_all x1, starting transfers between devices, per_device(): lax.all_to_all(outbound, 'expert', split_axis=1, concat_axis=1, tiled=True)  9.53 us
    dot_general x1, matrix products, per_device(): jnp.einsum('mslcf,lfd->mslcd', hidden, w_down, preferred_element_type=jnp...  6.72 us
    reshape x1, local copies, waits for them, and re-layouts, per_device(): partial_value.reshape(micro_count, expert_count, local_count * capacity, -1)  5.08 us
    reshape x1, local copies, waits for them, and re-layouts, per_device(): outgoing.reshape(micro_count, expert_count, local_count * capacity, -1)  4.4 us
  transfers between devices with their start and end apart: 2, of which 2 were waited for; matrix products, arithmetic and copies ran while one was open for 0% of the time, Pallas kernels for 0%

commit v1 on v0

v1 whole, which is shorter than its diff:
```python
import jax
import jax.numpy as jnp
from jax import lax
from jax.experimental import pallas as pl
from jax.experimental.pallas import tpu as pltpu
from jax.sharding import PartitionSpec as P

TOK = 16
TOP = 8
RING = 8
EXPERTS = 128
SLOTS = 256
WIDTH = 1024
HID = 192
DV = (0, 1, 7, 2, 6, 3, 5, 4)
GROUPS = 2
PAIRS_G = RING // GROUPS
ROWS_G = SLOTS // GROUPS
HALF_G = ROWS_G // 2
LAG = 2
MSG = WIDTH + 2 * SLOTS
F32 = jnp.float32
BF16 = jnp.bfloat16


def dot_nt(a, b):
    return lax.dot_general(a, b, (((1,), (1,)), ((), ())), preferred_element_type=F32)


def dot_nn(a, b):
    return lax.dot_general(a, b, (((1,), (0,)), ((), ())), preferred_element_type=F32)


def spread_matrix(u, v, c, su, sv):
    slot = lax.broadcasted_iota(jnp.int32, (SLOTS, 2 * EXPERTS), 0)
    column = lax.broadcasted_iota(jnp.int32, (SLOTS, 2 * EXPERTS), 1)
    pair = slot >> 5
    odd = pair & 1
    dv = jnp.where(odd == 1, (pair + 1) >> 1, (8 - (pair >> 1)) & 7)
    dc = (slot >> 4) & 1
    rank = slot & 1
    owner = u * su + ((dv + v) & 7) * sv + ((dc + c) & 1)
    return jnp.where(column == rank * EXPERTS + owner, 1.0, 0.0).astype(BF16)


def kernel(
    tok, routes, probs, wg, wu, wd, out,
    wgv, wuv, wdv, stg, outb, xb, mix_hi, mix_lo, hid, a_out, a_in, b_late, b_out, b_in, y_out, back, z_out, z_in,
    w_sem, s1s, s1r, s2s, s2r, xss, xsr, fws, fwr, ras, rar, rbs, rbr, s3s, s3r, s4s, s4r,
):
    e = lax.axis_index("expert")
    x = lax.axis_index("pair")
    c = e % 2
    y = (e // 2) % RING
    z = e // (2 * RING)
    right = (x + 1) % 4
    left = (x + 3) % 4

    def role(core):
        u = (1 - core) * z + core * y
        v = (1 - core) * y + core * z
        return u, v, 16 - 14 * core, 2 + 14 * core

    u, v, su, sv = role(c)

    loads = []
    for k in range(4):
        quarter = pl.ds(pl.multiple_of(((x + 4 - k) % 4) * WIDTH, WIDTH), WIDTH)
        for j, (src, dst) in enumerate(((wg, wgv), (wu, wuv), (wd, wdv))):
            copy = pltpu.make_async_copy(src.at[0, :, quarter], dst.at[k], w_sem.at[3 * k + j])
            copy.start()
            loads.append(copy)

    barrier = pltpu.get_barrier_semaphore()

    def greet(expert, pair):
        pl.semaphore_signal(barrier, inc=1, device_id=(expert, pair), device_id_type=pl.DeviceIdType.MESH)

    for d in range(1, RING):
        for core in range(2):
            greet(((z + d) % RING) * 16 + y * 2 + core, x)
            greet(z * 16 + ((y + d) % RING) * 2 + core, x)
    greet(z * 16 + y * 2 + (1 - c), x)
    greet(e, right)
    greet(e, left)

    prob = probs[...]
    mixing = prob / jnp.sum(prob, axis=1, keepdims=True)
    chosen = routes[...]
    lanes = lax.broadcasted_iota(jnp.int32, (TOK, EXPERTS), 1)
    mix = jnp.zeros((TOK, EXPERTS), F32)
    for k in range(TOP):
        mix = jnp.where(chosen[:, k:k + 1] == lanes, mixing[:, k:k + 1], mix)
    named = jnp.where(mix > 0, 1.0, 0.0)
    row = lax.broadcasted_iota(jnp.int32, (TOK, TOK), 0)
    col = lax.broadcasted_iota(jnp.int32, (TOK, TOK), 1)
    earlier = dot_nn(jnp.where(row > col, 1.0, 0.0).astype(BF16), named.astype(BF16))
    second = earlier > 0.5
    for r in range(2):
        part = jnp.where(second, mix, 0.0) if r else jnp.where(second, 0.0, mix)
        high = part.astype(BF16)
        low = (part - high.astype(F32)).astype(BF16)
        stg[0:TOK, WIDTH + r * EXPERTS:WIDTH + (r + 1) * EXPERTS] = high
        stg[0:TOK, WIDTH + SLOTS + r * EXPERTS:WIDTH + SLOTS + (r + 1) * EXPERTS] = low
    stg[0:TOK, 0:WIDTH] = tok[...]

    pl.semaphore_wait(barrier, 31)

    def remote(src, dst, send, recv, expert, pair):
        return pltpu.make_async_remote_copy(
            src_ref=src, dst_ref=dst, send_sem=send, recv_sem=recv,
            device_id=(expert, pair), device_id_type=pl.DeviceIdType.MESH,
        )

    gathers = []
    for du in (1, 7, 2, 6, 3, 5, 4):
        copy = remote(
            stg.at[0:TOK, :], stg.at[du * TOK:(du + 1) * TOK, :], s1s.at[du - 1], s1r.at[du - 1],
            ((u + du) % RING) * su + v * sv + c, x,
        )
        copy.start()
        gathers.append(copy)
    spread = spread_matrix(u, v, c, su, sv)
    for copy in gathers:
        copy.wait_recv()

    source = stg[:, WIDTH:WIDTH + SLOTS]
    tok_du = lax.broadcasted_iota(jnp.int32, (SLOTS, RING * TOK), 1) >> 4
    slot_du = (lax.broadcasted_iota(jnp.int32, (SLOTS, RING * TOK), 0) >> 1) & 7
    placing = jnp.where(jnp.logical_and(dot_nt(spread, source) > 0, tok_du == slot_du), 1.0, 0.0).astype(BF16)
    routed = [None] * 16
    for g in range(GROUPS):
        rows = dot_nn(placing[g * ROWS_G:(g + 1) * ROWS_G, :], stg[:, 0:WIDTH]).astype(BF16)
        outb[g * ROWS_G:(g + 1) * ROWS_G, :] = rows
        if g == 0:
            xb[0, 0:TOK, :] = rows[0:TOK, :]
        for i in range(g * PAIRS_G, (g + 1) * PAIRS_G):
            for dc in range(2):
                j = 2 * i + dc
                if j == 0:
                    continue
                copy = remote(
                    outb.at[j * 16:(j + 1) * 16, :], xb.at[0, j * 16:(j + 1) * 16, :], s2s.at[j], s2r.at[j],
                    u * su + ((v + DV[i]) % RING) * sv + (c + dc) % 2, x,
                )
                copy.start()
                routed[j] = copy

    tok_du = lax.broadcasted_iota(jnp.int32, (RING * TOK, SLOTS), 0) >> 4
    slot_du = (lax.broadcasted_iota(jnp.int32, (RING * TOK, SLOTS), 1) >> 1) & 7
    same = tok_du == slot_du
    mix_hi[...] = jnp.where(same, dot_nt(source, spread), 0.0).astype(BF16)
    mix_lo[...] = jnp.where(same, dot_nt(stg[:, WIDTH + SLOTS:MSG], spread), 0.0).astype(BF16)

    sent = [[None] * RING, [None] * RING]
    forwarded = [[None] * RING, [None] * RING]

    def send_pair(i):
        rows = slice(32 * i, 32 * i + 32)
        for dc in range(2):
            if 2 * i + dc:
                routed[2 * i + dc].wait_recv()
        for way, (k, target) in enumerate(((1, right), (3, left))):
            copy = remote(xb.at[0, rows, :], xb.at[k, rows, :], xss.at[way, i], xsr.at[way, i], e, target)
            copy.start()
            sent[way][i] = copy

    def forward_pair(i):
        for way, (k, target) in enumerate(((1, right), (3, left))):
            rows = slice(32 * i + 16 * way, 32 * i + 16 * way + 16)
            sent[way][i].wait_recv()
            copy = remote(xb.at[k, rows, :], xb.at[2, rows, :], fws.at[way, i], fwr.at[way, i], e, target)
            copy.start()
            forwarded[way][i] = copy

    def hidden(g):
        rows = slice(g * ROWS_G, (g + 1) * ROWS_G)
        for i in range(g * PAIRS_G, (g + 1) * PAIRS_G):
            for way in range(2):
                forwarded[way][i].wait_recv()
        gate = jnp.zeros((ROWS_G, HID), F32)
        up = jnp.zeros((ROWS_G, HID), F32)
        for k in range(4):
            gate = gate + dot_nt(xb[k, rows, :], wgv[k])
            up = up + dot_nt(xb[k, rows, :], wuv[k])
        hid[rows, :] = (gate / (1.0 + jnp.exp(-gate)) * up).astype(BF16)

    far = [None] * GROUPS
    near = [None] * GROUPS

    def down(g, k):
        return dot_nn(hid[g * ROWS_G:(g + 1) * ROWS_G, :], wdv[k])

    def halves(way):
        return slice(way * HALF_G, (way + 1) * HALF_G), slice((1 - way) * HALF_G, (2 - way) * HALF_G)

    def send_far(g):
        a_out[g] = down(g, 2).astype(BF16)
        far[g] = []
        for way, target in enumerate((right, left)):
            copy = remote(a_out.at[g, halves(way)[0], :], a_in.at[way, g], ras.at[way, g], rar.at[way, g], e, target)
            copy.start()
            far[g].append(copy)

    def send_near(way, g, rows, late):
        target = left if way else right
        copy = remote(
            b_out.at[way, g, rows, :], b_in.at[way, g, rows, :],
            rbs.at[way, g, late], rbr.at[way, g, late], e, target,
        )
        copy.start()
        near[g].append(copy)

    def send_near_free(g):
        near[g] = []
        for way, k in enumerate((3, 1)):
            late, free = halves(way)
            term = down(g, k)
            b_late[way, g] = term[late, :]
            b_out[way, g, free, :] = term[free, :].astype(BF16)
            send_near(way, g, free, 0)

    def send_near_late(g):
        for way in range(2):
            late, _ = halves(way)
            far[g][way].wait_recv()
            b_out[way, g, late, :] = (b_late[way, g] + a_in[way, g].astype(F32)).astype(BF16)
            send_near(way, g, late, 1)

    returned = [None] * 16

    def send_back(g):
        rows = slice(g * ROWS_G, (g + 1) * ROWS_G)
        term = down(g, 0)
        for copy in near[g]:
            copy.wait_recv()
        total = (term + b_in[0, g].astype(F32) + b_in[1, g].astype(F32)).astype(BF16)
        y_out[rows, :] = total
        if g == 0:
            back[0:TOK, :] = total[0:TOK, :]
        for i in range(g * PAIRS_G, (g + 1) * PAIRS_G):
            for dc in range(2):
                j = 2 * i + dc
                if j == 0:
                    continue
                core = (c + dc) % 2
                u_s, v_s, su_s, sv_s = role(core)
                copy = remote(
                    y_out.at[j * 16:(j + 1) * 16, :], back.at[j * 16:(j + 1) * 16, :], s3s.at[j], s3r.at[j],
                    u_s * su_s + ((v_s + RING - DV[i]) % RING) * sv_s + core, x,
                )
                copy.start()
                returned[j] = copy

    for i in range(RING):
        send_pair(i)
        if i >= LAG:
            forward_pair(i - LAG)
    for copy in loads:
        copy.wait()
    hidden(0)
    for i in range(RING - LAG, RING):
        forward_pair(i)
    send_far(0)
    send_near_free(0)
    for g in range(1, GROUPS):
        hidden(g)
        send_far(g)
        send_near_late(g - 1)
        send_near_free(g)
        send_back(g - 1)
    send_near_late(GROUPS - 1)
    send_back(GROUPS - 1)

    mixture = jnp.zeros((RING * TOK, WIDTH), F32)
    for g in range(GROUPS):
        rows = slice(g * ROWS_G, (g + 1) * ROWS_G)
        for j in range(g * 2 * PAIRS_G, (g + 1) * 2 * PAIRS_G):
            if j:
                returned[j].wait_recv()
        mixture = mixture + dot_nn(mix_hi[:, rows], back[rows, :]) + dot_nn(mix_lo[:, rows], back[rows, :])
    z_out[...] = mixture.astype(BF16)
    homes = []
    for du in (1, 7, 2, 6, 3, 5, 4):
        copy = remote(
            z_out.at[du * TOK:(du + 1) * TOK, :], z_in.at[du], s4s.at[du - 1], s4r.at[du - 1],
            ((u + RING - du) % RING) * su + v * sv + c, x,
        )
        copy.start()
        homes.append(copy)
    total = mixture[0:TOK, :]
    for du, copy in zip((1, 7, 2, 6, 3, 5, 4), homes):
        copy.wait_recv()
        total = total + z_in[du].astype(F32)
    out[...] = total.astype(BF16)

    for copy in gathers + routed[1:] + sum(sent + forwarded + far + near, []) + returned[1:] + homes:
        copy.wait_send()


def per_device(tokens, routes, router_probs, w_gate, w_up, w_down):
    vmem = pl.BlockSpec(memory_space=pltpu.VMEM)
    hbm = pl.BlockSpec(memory_space=pl.ANY)
    dma = pltpu.SemaphoreType.DMA
    return pl.pallas_call(
        kernel,
        out_shape=jax.ShapeDtypeStruct((TOK, WIDTH), BF16),
        in_specs=[vmem] * 3 + [hbm] * 3,
        out_specs=vmem,
        scratch_shapes=[
            pltpu.VMEM((4, HID, WIDTH), BF16),
            pltpu.VMEM((4, HID, WIDTH), BF16),
            pltpu.VMEM((4, HID, WIDTH), BF16),
            pltpu.VMEM((RING * TOK, MSG), BF16),
            pltpu.VMEM((SLOTS, WIDTH), BF16),
            pltpu.VMEM((4, SLOTS, WIDTH), BF16),
            pltpu.VMEM((RING * TOK, SLOTS), BF16),
            pltpu.VMEM((RING * TOK, SLOTS), BF16),
            pltpu.VMEM((SLOTS, HID), BF16),
            pltpu.VMEM((GROUPS, ROWS_G, WIDTH), BF16),
            pltpu.VMEM((2, GROUPS, HALF_G, WIDTH), BF16),
            pltpu.VMEM((2, GROUPS, HALF_G, WIDTH), F32),
            pltpu.VMEM((2, GROUPS, ROWS_G, WIDTH), BF16),
            pltpu.VMEM((2, GROUPS, ROWS_G, WIDTH), BF16),
            pltpu.VMEM((SLOTS, WIDTH), BF16),
            pltpu.VMEM((SLOTS, WIDTH), BF16),
            pltpu.VMEM((RING * TOK, WIDTH), BF16),
            pltpu.VMEM((RING, TOK, WIDTH), BF16),
            dma((12,)),
            dma((7,)), dma((7,)),
            dma((16,)), dma((16,)),
            dma((2, RING)), dma((2, RING)),
            dma((2, RING)), dma((2, RING)),
            dma((2, GROUPS)), dma((2, GROUPS)),
            dma((2, GROUPS, 2)), dma((2, GROUPS, 2)),
            dma((16,)), dma((16,)),
            dma((7,)), dma((7,)),
        ],
        compiler_params=pltpu.CompilerParams(
            collective_id=0, has_side_effects=True, vmem_limit_bytes=48 * 1024 * 1024
        ),
    )(tokens, routes, router_probs, w_gate, w_up, w_down)


def solution(mesh):
    in_specs = (
        P("expert", "pair"),
        P("expert", None),
        P("expert", None),
        P("expert", "pair", None),
        P("expert", "pair", None),
        P("expert", "pair", None),
    )
    out_specs = P("expert", "pair")
    return jax.shard_map(
        per_device, mesh=mesh, in_specs=in_specs, out_specs=out_specs, check_vma=False
    )
```

time: 210 us -> 87.3 us (0.42)
  blocking collectives: 82.4 us -> 0 us
  Pallas kernels: 0 us -> 79.8 us
  waiting for transfers between devices: 69.3 us -> 0 us
  local copies, waits for them, and re-layouts: 21 us -> 7.11 us
  between operations: 13.5 us -> 0.01 us
  matrix products: 11.8 us -> 0 us
  starting transfers between devices: 9.79 us -> 0 us
    pallas_call x0 -> x1, Pallas kernels: none -> 79.8 us  [per_device(): pl.pallas_call(kernel, out_shape=jax.ShapeDtypeStruct((TOK, WIDTH), BF16)...]
    all_to_all x1 -> x0, blocking collectives: 71.9 us -> none  [per_device(): lax.all_to_all(outgoing, 'expert', split_axis=1, concat_axis=1, tiled=True)]
    all_to_all x1 -> x0, waiting for transfers between devices: 50.4 us -> none  [per_device(): lax.all_to_all(outbound, 'expert', split_axis=1, concat_axis=1, tiled=True)]
    reduce_scatter x1 -> x0, waiting for transfers between devices: 18.9 us -> none  [per_device(): lax.psum_scatter(mixture.reshape(tok_rows, -1).astype(jnp.bfloat16), 'pai...]
    reshape x3 -> x0, local copies, waits for them, and re-layouts: 13.6 us -> none  [the longest x1 5.08 us: per_device(): partial_value.reshape(micro_count, expert_count, local_count * capacity, -1)]
    dot_general x4 -> x0, matrix products: 11.8 us -> none  [the longest x1 6.72 us: per_device(): jnp.einsum('mslcf,lfd->mslcd', hidden, w_down, preferred_element_type=jnp...]
    all_gather x1 -> x0, blocking collectives: 10.5 us -> none  [per_device(): gathered = lax.all_gather(tokens, 'pair', axis=1, tiled=True)]
    all_to_all x1 -> x0, starting transfers between devices: 9.53 us -> none  [per_device(): lax.all_to_all(outbound, 'expert', split_axis=1, concat_axis=1, tiled=True)]
  transfers between devices with their start and end apart: 2 -> 0, of which waited for: 2 -> 0; matrix products, arithmetic and copies ran while one was open for 0% -> 0% of each run, Pallas kernels for 0% -> 0%
where the time goes in v1:
time: 87.3 us; the launch traced here: 87 us
  Pallas kernels  79.8 us (91%)
  local copies, waits for them, and re-layouts  7.11 us (8%)
    pallas_call x1, Pallas kernels, per_device(): pl.pallas_call(kernel, out_shape=jax.ShapeDtypeStruct((TOK, WIDTH), BF16)...  79.8 us
    unnamed x11, local copies, waits for them, and re-layouts  7.11 us

profile of v1, /device:TPU:1, one launch (start us, length us, event | category | flops | bytes accessed | tf_op | source)
XLA Modules:
  0.0 87.0 jit_solution(9901420341924022697)
XLA Ops:
  0.0 0.8 copy.7.routes
  0.8 0.8 copy.8.probs
  1.5 0.0 copy-start
  1.5 1.4 %copy-done = bf16[1,192,4096]{2,1,0:T(8,128)(2,1)S(1)} copy-done((bf16[1,192,4096]{2,1,0:T(8,128)(2,1)S(1)}, bf16[1,192,4096]{2,1,0:T(8,128)(2,1)}, u32[]{:S(2)}) %copy-start) | copy-done | bytes 1572888
  2.9 0.0 copy-start.1
  2.9 1.4 %copy-done.1 = bf16[1,192,4096]{2,1,0:T(8,128)(2,1)S(1)} copy-done((bf16[1,192,4096]{2,1,0:T(8,128)(2,1)S(1)}, bf16[1,192,4096]{2,1,0:T(8,128)(2,1)}, u32[]{:S(2)}) %copy-start.1) | copy-done | bytes 1572888
  4.3 0.0 copy-start.2
  4.3 1.4 %copy-done.2 = bf16[1,192,4096]{2,1,0:T(8,128)(2,1)S(1)} copy-done((bf16[1,192,4096]{2,1,0:T(8,128)(2,1)S(1)}, bf16[1,192,4096]{2,1,0:T(8,128)(2,1)}, u32[]{:S(2)}) %copy-start.2) | copy-done | bytes 1572888
  5.7 0.0 copy-start.3
  5.7 0.8 copy-done.3
  6.5 79.8 %shard_map.64 = bf16[16,1024]{1,0:T(8,128)(2,1)S(1)} custom-call(bf16[16,1024]{1,0:T(8,128)(2,1)S(1)} %copy-done.3, s32[16,8]{1,0:T(8,128)S(1)} %copy.7.routes, f32[16,8]{1,0:T(8,128)S(1)} %copy.8.probs, bf16[1,192,4096]{2,1,0:T(8,128)(2,1)S(1)} %copy-done, bf16[1,192,4096]{2,1,0:T(8,128)(2,1)S(1)} %copy-done.1, bf16[1,192,4096]{2,1,0:T(8,128)(2,1)S(1)} %copy-done.2), custom_call_target="tpu_custom_call" | custom-call | tf_op jit(solution)/shard_map/pallas_call | solution.py:305
  86.4 0.6 copy.10
Async XLA Ops:
  1.5 1.4 %copy-start = (bf16[1,192,4096]{2,1,0:T(8,128)(2,1)S(1)}, bf16[1,192,4096]{2,1,0:T(8,128)(2,1)}, u32[]{:S(2)}) copy-start(bf16[1,192,4096]{2,1,0:T(8,128)(2,1)} %wg.1) | copy-start | bytes 4718596
  2.9 1.4 %copy-start.1 = (bf16[1,192,4096]{2,1,0:T(8,128)(2,1)S(1)}, bf16[1,192,4096]{2,1,0:T(8,128)(2,1)}, u32[]{:S(2)}) copy-start(bf16[1,192,4096]{2,1,0:T(8,128)(2,1)} %wu.1) | copy-start | bytes 4718596
  4.3 1.4 %copy-start.2 = (bf16[1,192,4096]{2,1,0:T(8,128)(2,1)S(1)}, bf16[1,192,4096]{2,1,0:T(8,128)(2,1)}, u32[]{:S(2)}) copy-start(bf16[1,192,4096]{2,1,0:T(8,128)(2,1)} %wd.1) | copy-start | bytes 4718596
  5.7 0.8 copy-start.3

commit v2 on v1

--- a/solution.py
+++ b/solution.py
@@ -18,7 +18,8 @@
 ROWS_G = SLOTS // GROUPS
 HALF_G = ROWS_G // 2
 LAG = 2
-MSG = WIDTH + 2 * SLOTS
+MSG = WIDTH + 128
+FAR_FIRST = (4, 3, 5, 2, 6, 1, 7)
 F32 = jnp.float32
 BF16 = jnp.bfloat16
 
@@ -31,22 +32,18 @@
     return lax.dot_general(a, b, (((1,), (0,)), ((), ())), preferred_element_type=F32)
 
 
-def spread_matrix(u, v, c, su, sv):
-    slot = lax.broadcasted_iota(jnp.int32, (SLOTS, 2 * EXPERTS), 0)
-    column = lax.broadcasted_iota(jnp.int32, (SLOTS, 2 * EXPERTS), 1)
-    pair = slot >> 5
-    odd = pair & 1
-    dv = jnp.where(odd == 1, (pair + 1) >> 1, (8 - (pair >> 1)) & 7)
-    dc = (slot >> 4) & 1
-    rank = slot & 1
-    owner = u * su + ((dv + v) & 7) * sv + ((dc + c) & 1)
-    return jnp.where(column == rank * EXPERTS + owner, 1.0, 0.0).astype(BF16)
+def iota(shape, dim):
+    return lax.broadcasted_iota(jnp.int32, shape, dim)
+
+
+def ones_where(condition):
+    return jnp.where(condition, 1.0, 0.0).astype(BF16)
 
 
 def kernel(
-    tok, routes, probs, wg, wu, wd, out,
-    wgv, wuv, wdv, stg, outb, xb, mix_hi, mix_lo, hid, a_out, a_in, b_late, b_out, b_in, y_out, back, z_out, z_in,
-    w_sem, s1s, s1r, s2s, s2r, xss, xsr, fws, fwr, ras, rar, rbs, rbr, s3s, s3r, s4s, s4r,
+    tok_hbm, routes_hbm, probs_hbm, wg, wu, wd, out,
+    routes, probs, wgv, wuv, wdv, pieces, snd, stg, outb, xb, mix_hi, mix_lo, hid, a_out, a_in, b_late, b_out, b_in, y_out, back, z_out, z_in,
+    in_sem, w_sem, s1s, s1r, s2s, s2r, xss, xsr, fws, fwr, ras, rar, rbs, rbr, s3s, s3r, s4s, s4r,
 ):
     e = lax.axis_index("expert")
     x = lax.axis_index("pair")
@@ -63,6 +60,29 @@
 
     u, v, su, sv = role(c)
 
+    barrier = pltpu.get_barrier_semaphore()
+
+    def greet(expert, pair):
+        pl.semaphore_signal(barrier, inc=1, device_id=(expert, pair), device_id_type=pl.DeviceIdType.MESH)
+
+    for d in FAR_FIRST:
+        for core in range(2):
+            greet(((z + d) % RING) * 16 + y * 2 + core, x)
+            greet(z * 16 + ((y + d) % RING) * 2 + core, x)
+    greet(z * 16 + y * 2 + (1 - c), x)
+    greet(e, right)
+    greet(e, left)
+
+    inputs = [
+        pltpu.make_async_copy(routes_hbm, routes, in_sem.at[8]),
+        pltpu.make_async_copy(probs_hbm, probs, in_sem.at[9]),
+        pltpu.make_async_copy(tok_hbm, stg.at[0:TOK, 0:WIDTH], in_sem.at[0]),
+    ]
+    for du in FAR_FIRST:
+        inputs.append(pltpu.make_async_copy(tok_hbm, snd.at[du, :, 0:WIDTH], in_sem.at[du]))
+    for copy in inputs:
+        copy.start()
+
     loads = []
     for k in range(4):
         quarter = pl.ds(pl.multiple_of(((x + 4 - k) % 4) * WIDTH, WIDTH), WIDTH)
@@ -71,38 +91,38 @@
             copy.start()
             loads.append(copy)
 
-    barrier = pltpu.get_barrier_semaphore()
-
-    def greet(expert, pair):
-        pl.semaphore_signal(barrier, inc=1, device_id=(expert, pair), device_id_type=pl.DeviceIdType.MESH)
-
-    for d in range(1, RING):
-        for core in range(2):
-            greet(((z + d) % RING) * 16 + y * 2 + core, x)
-            greet(z * 16 + ((y + d) % RING) * 2 + core, x)
-    greet(z * 16 + y * 2 + (1 - c), x)
-    greet(e, right)
-    greet(e, left)
-
+    inputs[0].wait()
+    inputs[1].wait()
     prob = probs[...]
-    mixing = prob / jnp.sum(prob, axis=1, keepdims=True)
+    mixing = prob / jnp.sum(prob, axis=0, keepdims=True)
     chosen = routes[...]
-    lanes = lax.broadcasted_iota(jnp.int32, (TOK, EXPERTS), 1)
-    mix = jnp.zeros((TOK, EXPERTS), F32)
+    experts = iota((EXPERTS, TOK), 0)
+    mix = jnp.zeros((EXPERTS, TOK), F32)
     for k in range(TOP):
-        mix = jnp.where(chosen[:, k:k + 1] == lanes, mixing[:, k:k + 1], mix)
-    named = jnp.where(mix > 0, 1.0, 0.0)
-    row = lax.broadcasted_iota(jnp.int32, (TOK, TOK), 0)
-    col = lax.broadcasted_iota(jnp.int32, (TOK, TOK), 1)
-    earlier = dot_nn(jnp.where(row > col, 1.0, 0.0).astype(BF16), named.astype(BF16))
-    second = earlier > 0.5
+        mix = jnp.where(chosen[k:k + 1, :] == experts, mixing[k:k + 1, :], mix)
+    named = jnp.where(mix > 0, 1.0, 0.0).astype(BF16)
+    row, col = iota((TOK, TOK), 0), iota((TOK, TOK), 1)
+    second = dot_nn(named, ones_where(row < col)) > 0.5
+    same_token = ones_where(row == col)
     for r in range(2):
         part = jnp.where(second, mix, 0.0) if r else jnp.where(second, 0.0, mix)
         high = part.astype(BF16)
         low = (part - high.astype(F32)).astype(BF16)
-        stg[0:TOK, WIDTH + r * EXPERTS:WIDTH + (r + 1) * EXPERTS] = high
-        stg[0:TOK, WIDTH + SLOTS + r * EXPERTS:WIDTH + SLOTS + (r + 1) * EXPERTS] = low
-    stg[0:TOK, 0:WIDTH] = tok[...]
+        for j, piece in enumerate((high, low)):
+            start = (2 * j + r) * EXPERTS
+            pieces[:, start:start + EXPERTS] = dot_nt(same_token, piece).astype(BF16)
+    lane = iota((RING * 128, 1), 0)
+    pair = (lane >> 2) & 7
+    offset = jnp.where((pair & 1) == 1, (pair + 1) >> 1, (8 - (pair >> 1)) & 7)
+    owner = ((u + (lane >> 7)) & 7) * su + ((v + offset) & 7) * sv + ((c + (lane >> 1)) & 1)
+    column = ((lane >> 5) & 3) * 2 * EXPERTS + (lane & 1) * EXPERTS + owner
+    pick = ones_where(iota((RING * 128, 4 * EXPERTS), 1) == column)
+    blocks = dot_nt(pieces[...], pick).astype(BF16)
+    stg[0:TOK, WIDTH:MSG] = blocks[:, 0:128]
+    for du in range(1, RING):
+        snd[du, :, WIDTH:MSG] = blocks[:, du * 128:(du + 1) * 128]
+    for copy in inputs[2:]:
+        copy.wait()
 
     pl.semaphore_wait(barrier, 31)
 
@@ -113,21 +133,22 @@
         )
 
     gathers = []
-    for du in (1, 7, 2, 6, 3, 5, 4):
+    for du in FAR_FIRST:
         copy = remote(
-            stg.at[0:TOK, :], stg.at[du * TOK:(du + 1) * TOK, :], s1s.at[du - 1], s1r.at[du - 1],
+            snd.at[du], stg.at[du * TOK:(du + 1) * TOK, :], s1s.at[du - 1], s1r.at[du - 1],
             ((u + du) % RING) * su + v * sv + c, x,
         )
         copy.start()
         gathers.append(copy)
-    spread = spread_matrix(u, v, c, su, sv)
+    slot = iota((SLOTS, 128), 0)
+    spread = [ones_where(iota((SLOTS, 128), 1) == 32 * j + ((slot >> 4) << 1) + (slot & 1)) for j in range(2)]
     for copy in gathers:
         copy.wait_recv()
 
-    source = stg[:, WIDTH:WIDTH + SLOTS]
-    tok_du = lax.broadcasted_iota(jnp.int32, (SLOTS, RING * TOK), 1) >> 4
-    slot_du = (lax.broadcasted_iota(jnp.int32, (SLOTS, RING * TOK), 0) >> 1) & 7
-    placing = jnp.where(jnp.logical_and(dot_nt(spread, source) > 0, tok_du == slot_du), 1.0, 0.0).astype(BF16)
+    source = stg[:, WIDTH:MSG]
+    tok_du = iota((SLOTS, RING * TOK), 1) >> 4
+    slot_du = (iota((SLOTS, RING * TOK), 0) >> 1) & 7
+    placing = ones_where(jnp.logical_and(dot_nt(spread[0], source) > 0, tok_du == slot_du))
     routed = [None] * 16
     for g in range(GROUPS):
         rows = dot_nn(placing[g * ROWS_G:(g + 1) * ROWS_G, :], stg[:, 0:WIDTH]).astype(BF16)
@@ -146,11 +167,11 @@
                 copy.start()
                 routed[j] = copy
 
-    tok_du = lax.broadcasted_iota(jnp.int32, (RING * TOK, SLOTS), 0) >> 4
-    slot_du = (lax.broadcasted_iota(jnp.int32, (RING * TOK, SLOTS), 1) >> 1) & 7
+    tok_du = iota((RING * TOK, SLOTS), 0) >> 4
+    slot_du = (iota((RING * TOK, SLOTS), 1) >> 1) & 7
     same = tok_du == slot_du
-    mix_hi[...] = jnp.where(same, dot_nt(source, spread), 0.0).astype(BF16)
-    mix_lo[...] = jnp.where(same, dot_nt(stg[:, WIDTH + SLOTS:MSG], spread), 0.0).astype(BF16)
+    mix_hi[...] = jnp.where(same, dot_nt(source, spread[0]), 0.0).astype(BF16)
+    mix_lo[...] = jnp.where(same, dot_nt(source, spread[1]), 0.0).astype(BF16)
 
     sent = [[None] * RING, [None] * RING]
     forwarded = [[None] * RING, [None] * RING]
@@ -281,7 +302,7 @@
         mixture = mixture + dot_nn(mix_hi[:, rows], back[rows, :]) + dot_nn(mix_lo[:, rows], back[rows, :])
     z_out[...] = mixture.astype(BF16)
     homes = []
-    for du in (1, 7, 2, 6, 3, 5, 4):
+    for du in FAR_FIRST:
         copy = remote(
             z_out.at[du * TOK:(du + 1) * TOK, :], z_in.at[du], s4s.at[du - 1], s4r.at[du - 1],
             ((u + RING - du) % RING) * su + v * sv + c, x,
@@ -289,7 +310,7 @@
         copy.start()
         homes.append(copy)
     total = mixture[0:TOK, :]
-    for du, copy in zip((1, 7, 2, 6, 3, 5, 4), homes):
+    for du, copy in zip(FAR_FIRST, homes):
         copy.wait_recv()
         total = total + z_in[du].astype(F32)
     out[...] = total.astype(BF16)
@@ -300,17 +321,21 @@
 
 def per_device(tokens, routes, router_probs, w_gate, w_up, w_down):
     vmem = pl.BlockSpec(memory_space=pltpu.VMEM)
-    hbm = pl.BlockSpec(memory_space=pl.ANY)
+    hbm = pl.BlockSpec(memory_space=pltpu.HBM)
     dma = pltpu.SemaphoreType.DMA
     return pl.pallas_call(
         kernel,
         out_shape=jax.ShapeDtypeStruct((TOK, WIDTH), BF16),
-        in_specs=[vmem] * 3 + [hbm] * 3,
+        in_specs=[hbm] * 6,
         out_specs=vmem,
         scratch_shapes=[
+            pltpu.VMEM((TOP, TOK), jnp.int32),
+            pltpu.VMEM((TOP, TOK), F32),
             pltpu.VMEM((4, HID, WIDTH), BF16),
             pltpu.VMEM((4, HID, WIDTH), BF16),
             pltpu.VMEM((4, HID, WIDTH), BF16),
+            pltpu.VMEM((TOK, 4 * EXPERTS), BF16),
+            pltpu.VMEM((RING, TOK, MSG), BF16),
             pltpu.VMEM((RING * TOK, MSG), BF16),
             pltpu.VMEM((SLOTS, WIDTH), BF16),
             pltpu.VMEM((4, SLOTS, WIDTH), BF16),
@@ -326,6 +351,7 @@
             pltpu.VMEM((SLOTS, WIDTH), BF16),
             pltpu.VMEM((RING * TOK, WIDTH), BF16),
             pltpu.VMEM((RING, TOK, WIDTH), BF16),
+            dma((10,)),
             dma((12,)),
             dma((7,)), dma((7,)),
             dma((16,)), dma((16,)),
@@ -337,9 +363,9 @@
             dma((7,)), dma((7,)),
         ],
         compiler_params=pltpu.CompilerParams(
-            collective_id=0, has_side_effects=True, vmem_limit_bytes=48 * 1024 * 1024
+            collective_id=0, has_side_effects=True, vmem_limit_bytes=62 * 1024 * 1024
         ),
-    )(tokens, routes, router_probs, w_gate, w_up, w_down)
+    )(tokens, routes.T, router_probs.T, w_gate, w_up, w_down)
 
 
 def solution(mesh):

time: 87.3 us -> 78.9 us (0.904)
  local copies, waits for them, and re-layouts: 7.11 us -> 1.38 us
  Pallas kernels: 79.8 us -> 77.3 us
    unnamed x11 -> x1, local copies, waits for them, and re-layouts: 7.11 us -> 1.38 us
    pallas_call x1, Pallas kernels: 79.8 us -> 77.3 us  [per_device(): pl.pallas_call(kernel, out_shape=jax.ShapeDtypeStruct((TOK, WIDTH), BF16)...]
where the time goes in v2:
time: 78.9 us; the launch traced here: 78.7 us
  Pallas kernels  77.3 us (98%)
  local copies, waits for them, and re-layouts  1.38 us (2%)
    pallas_call x1, Pallas kernels, per_device(): pl.pallas_call(kernel, out_shape=jax.ShapeDtypeStruct((TOK, WIDTH), BF16)...  77.3 us

profile of v2, /device:TPU:1, one launch (start us, length us, event | category | flops | bytes accessed | tf_op | source)
XLA Modules:
  0.0 78.7 jit_solution(14935962172903370753)
XLA Ops:
  0.0 77.3 %shard_map.64 = bf16[16,1024]{1,0:T(8,128)(2,1)} custom-call(bf16[16,1024]{1,0:T(8,128)(2,1)} %tok_hbm.1, s32[8,16]{1,0:T(8,128)} %bitcast.2, f32[8,16]{1,0:T(8,128)} %bitcast.3, bf16[1,192,4096]{2,1,0:T(8,128)(2,1)} %wg.1, bf16[1,192,4096]{2,1,0:T(8,128)(2,1)} %wu.1, bf16[1,192,4096]{2,1,0:T(8,128)(2,1)} %wd.1), custom_call_target="tpu_custom_call" | custom-call | tf_op jit(solution)/shard_map/pallas_call | solution.py:326
  77.4 1.4 %copy.8 = bf16[16,1024]{1,0:T(8,128)(2,1)} copy(bf16[16,1024]{1,0:T(8,128)(2,1)} %shard_map.64) | data formatting | bytes 65536

commit v3 on v2

--- a/solution.py
+++ b/solution.py
@@ -18,7 +18,10 @@
 ROWS_G = SLOTS // GROUPS
 HALF_G = ROWS_G // 2
 LAG = 2
+EARLY_AFTER = 3
 MSG = WIDTH + 128
+EARLY = 384
+LATE = WIDTH - EARLY
 FAR_FIRST = (4, 3, 5, 2, 6, 1, 7)
 F32 = jnp.float32
 BF16 = jnp.bfloat16
@@ -42,8 +45,10 @@
 
 def kernel(
     tok_hbm, routes_hbm, probs_hbm, wg, wu, wd, out,
-    routes, probs, wgv, wuv, wdv, pieces, snd, stg, outb, xb, mix_hi, mix_lo, hid, a_out, a_in, b_late, b_out, b_in, y_out, back, z_out, z_in,
+    routes, probs, wgv, wuv, wdv, pieces, snd, stg, outb, own, ring, mix_hi, mix_lo, hid,
+    a_out, a_in, b_late, b_out, b_in, y_out, back, z_out, z_in, early_tok, early_out, early, early_y, early_back, early_z, early_sum,
     in_sem, w_sem, s1s, s1r, s2s, s2r, xss, xsr, fws, fwr, ras, rar, rbs, rbr, s3s, s3r, s4s, s4r,
+    ets, etr, ers, err, eys, eyr, ezs, ezr,
 ):
     e = lax.axis_index("expert")
     x = lax.axis_index("pair")
@@ -70,8 +75,8 @@
             greet(((z + d) % RING) * 16 + y * 2 + core, x)
             greet(z * 16 + ((y + d) % RING) * 2 + core, x)
     greet(z * 16 + y * 2 + (1 - c), x)
-    greet(e, right)
-    greet(e, left)
+    for k in range(1, 4):
+        greet(e, (x + k) % 4)
 
     inputs = [
         pltpu.make_async_copy(routes_hbm, routes, in_sem.at[8]),
@@ -124,7 +129,7 @@
     for copy in inputs[2:]:
         copy.wait()
 
-    pl.semaphore_wait(barrier, 31)
+    pl.semaphore_wait(barrier, 32)
 
     def remote(src, dst, send, recv, expert, pair):
         return pltpu.make_async_remote_copy(
@@ -145,27 +150,46 @@
     for copy in gathers:
         copy.wait_recv()
 
+    crossing = [None] * 3
+    for k in (2, 1, 3):
+        copy = remote(
+            stg.at[:, LATE:WIDTH], early_tok.at[:, (k - 1) * EARLY:k * EARLY], ets.at[k - 1], etr.at[k - 1], e, (x + k) % 4
+        )
+        copy.start()
+        crossing[k - 1] = copy
+
     source = stg[:, WIDTH:MSG]
     tok_du = iota((SLOTS, RING * TOK), 1) >> 4
     slot_du = (iota((SLOTS, RING * TOK), 0) >> 1) & 7
     placing = ones_where(jnp.logical_and(dot_nt(spread[0], source) > 0, tok_du == slot_du))
     routed = [None] * 16
+    routed_early = [None] * 16
+
+    def owner_of(j):
+        return u * su + ((v + DV[j // 2]) % RING) * sv + (c + j % 2) % 2
+
+    def rows_of(j):
+        return slice(j * 16, (j + 1) * 16)
+
+    def route_early():
+        for copy in crossing:
+            copy.wait_recv()
+        early_out[...] = dot_nn(placing, early_tok[...]).astype(BF16)
+        early[0:TOK, :] = early_out[0:TOK, :]
+        for j in range(1, 16):
+            copy = remote(early_out.at[rows_of(j), :], early.at[rows_of(j), :], ers.at[j], err.at[j], owner_of(j), x)
+            copy.start()
+            routed_early[j] = copy
+
     for g in range(GROUPS):
         rows = dot_nn(placing[g * ROWS_G:(g + 1) * ROWS_G, :], stg[:, 0:WIDTH]).astype(BF16)
         outb[g * ROWS_G:(g + 1) * ROWS_G, :] = rows
         if g == 0:
-            xb[0, 0:TOK, :] = rows[0:TOK, :]
-        for i in range(g * PAIRS_G, (g + 1) * PAIRS_G):
-            for dc in range(2):
-                j = 2 * i + dc
-                if j == 0:
-                    continue
-                copy = remote(
-                    outb.at[j * 16:(j + 1) * 16, :], xb.at[0, j * 16:(j + 1) * 16, :], s2s.at[j], s2r.at[j],
-                    u * su + ((v + DV[i]) % RING) * sv + (c + dc) % 2, x,
-                )
-                copy.start()
-                routed[j] = copy
+            own[0:TOK, :] = rows[0:TOK, :]
+        for j in range(max(1, g * 2 * PAIRS_G), (g + 1) * 2 * PAIRS_G):
+            copy = remote(outb.at[rows_of(j), :], own.at[rows_of(j), :], s2s.at[j], s2r.at[j], owner_of(j), x)
+            copy.start()
+            routed[j] = copy
 
     tok_du = iota((RING * TOK, SLOTS), 0) >> 4
     slot_du = (iota((RING * TOK, SLOTS), 1) >> 1) & 7
@@ -182,7 +206,7 @@
             if 2 * i + dc:
                 routed[2 * i + dc].wait_recv()
         for way, (k, target) in enumerate(((1, right), (3, left))):
-            copy = remote(xb.at[0, rows, :], xb.at[k, rows, :], xss.at[way, i], xsr.at[way, i], e, target)
+            copy = remote(own.at[rows, 0:LATE], ring.at[k - 1, rows, :], xss.at[way, i], xsr.at[way, i], e, target)
             copy.start()
             sent[way][i] = copy
 
@@ -190,7 +214,7 @@
         for way, (k, target) in enumerate(((1, right), (3, left))):
             rows = slice(32 * i + 16 * way, 32 * i + 16 * way + 16)
             sent[way][i].wait_recv()
-            copy = remote(xb.at[k, rows, :], xb.at[2, rows, :], fws.at[way, i], fwr.at[way, i], e, target)
+            copy = remote(ring.at[k - 1, rows, :], ring.at[1, rows, :], fws.at[way, i], fwr.at[way, i], e, target)
             copy.start()
             forwarded[way][i] = copy
 
@@ -199,18 +223,44 @@
         for i in range(g * PAIRS_G, (g + 1) * PAIRS_G):
             for way in range(2):
                 forwarded[way][i].wait_recv()
-        gate = jnp.zeros((ROWS_G, HID), F32)
-        up = jnp.zeros((ROWS_G, HID), F32)
-        for k in range(4):
-            gate = gate + dot_nt(xb[k, rows, :], wgv[k])
-            up = up + dot_nt(xb[k, rows, :], wuv[k])
+        for j in range(max(1, g * 2 * PAIRS_G), (g + 1) * 2 * PAIRS_G):
+            routed_early[j].wait_recv()
+
+        def product(weights):
+            total = dot_nt(own[rows, :], weights[0])
+            for k in range(1, 4):
+                total = total + dot_nt(ring[k - 1, rows, :], weights[k, :, 0:LATE])
+                total = total + dot_nt(early[rows, (k - 1) * EARLY:k * EARLY], weights[k, :, LATE:WIDTH])
+            return total
+
+        gate = product(wgv)
+        up = product(wuv)
         hid[rows, :] = (gate / (1.0 + jnp.exp(-gate)) * up).astype(BF16)
 
     far = [None] * GROUPS
     near = [None] * GROUPS
 
-    def down(g, k):
-        return dot_nn(hid[g * ROWS_G:(g + 1) * ROWS_G, :], wdv[k])
+    def down(g, k, lanes=slice(0, LATE)):
+        return dot_nn(hid[g * ROWS_G:(g + 1) * ROWS_G, :], wdv[k, :, lanes])
+
+    def source_of(j):
+        core = (c + j % 2) % 2
+        u_s, v_s, su_s, sv_s = role(core)
+        return u_s * su_s + ((v_s + RING - DV[j // 2]) % RING) * sv_s + core
+
+    returned = [None] * 16
+    returned_early = [None] * 16
+
+    def send_back_early(g):
+        rows = slice(g * ROWS_G, (g + 1) * ROWS_G)
+        for k in range(1, 4):
+            early_y[rows, (k - 1) * EARLY:k * EARLY] = down(g, k, slice(LATE, WIDTH)).astype(BF16)
+        if g == 0:
+            early_back[0:TOK, :] = early_y[0:TOK, :]
+        for j in range(max(1, g * 2 * PAIRS_G), (g + 1) * 2 * PAIRS_G):
+            copy = remote(early_y.at[rows_of(j), :], early_back.at[rows_of(j), :], eys.at[j], eyr.at[j], source_of(j), x)
+            copy.start()
+            returned_early[j] = copy
 
     def halves(way):
         return slice(way * HALF_G, (way + 1) * HALF_G), slice((1 - way) * HALF_G, (2 - way) * HALF_G)
@@ -248,49 +298,56 @@
             b_out[way, g, late, :] = (b_late[way, g] + a_in[way, g].astype(F32)).astype(BF16)
             send_near(way, g, late, 1)
 
-    returned = [None] * 16
-
     def send_back(g):
         rows = slice(g * ROWS_G, (g + 1) * ROWS_G)
         term = down(g, 0)
+        y_out[rows, LATE:WIDTH] = down(g, 0, slice(LATE, WIDTH)).astype(BF16)
         for copy in near[g]:
             copy.wait_recv()
-        total = (term + b_in[0, g].astype(F32) + b_in[1, g].astype(F32)).astype(BF16)
-        y_out[rows, :] = total
+        y_out[rows, 0:LATE] = (term + b_in[0, g].astype(F32) + b_in[1, g].astype(F32)).astype(BF16)
         if g == 0:
-            back[0:TOK, :] = total[0:TOK, :]
-        for i in range(g * PAIRS_G, (g + 1) * PAIRS_G):
-            for dc in range(2):
-                j = 2 * i + dc
-                if j == 0:
-                    continue
-                core = (c + dc) % 2
-                u_s, v_s, su_s, sv_s = role(core)
-                copy = remote(
-                    y_out.at[j * 16:(j + 1) * 16, :], back.at[j * 16:(j + 1) * 16, :], s3s.at[j], s3r.at[j],
-                    u_s * su_s + ((v_s + RING - DV[i]) % RING) * sv_s + core, x,
-                )
-                copy.start()
-                returned[j] = copy
+            back[0:TOK, :] = y_out[0:TOK, :]
+        for j in range(max(1, g * 2 * PAIRS_G), (g + 1) * 2 * PAIRS_G):
+            copy = remote(y_out.at[rows_of(j), :], back.at[rows_of(j), :], s3s.at[j], s3r.at[j], source_of(j), x)
+            copy.start()
+            returned[j] = copy
+
+    summed_early = [None] * 3
+
+    def send_sums_early():
+        for copy in returned_early[1:]:
+            copy.wait_recv()
+        early_z[...] = (dot_nn(mix_hi[...], early_back[...]) + dot_nn(mix_lo[...], early_back[...])).astype(BF16)
+        for k in (2, 1, 3):
+            copy = remote(
+                early_z.at[:, (k - 1) * EARLY:k * EARLY], early_sum.at[k - 1], ezs.at[k - 1], ezr.at[k - 1], e, (x + 4 - k) % 4
+            )
+            copy.start()
+            summed_early[k - 1] = copy
 
     for i in range(RING):
         send_pair(i)
         if i >= LAG:
             forward_pair(i - LAG)
+        if i == EARLY_AFTER:
+            route_early()
     for copy in loads:
         copy.wait()
     hidden(0)
     for i in range(RING - LAG, RING):
         forward_pair(i)
     send_far(0)
+    send_back_early(0)
     send_near_free(0)
     for g in range(1, GROUPS):
         hidden(g)
         send_far(g)
+        send_back_early(g)
         send_near_late(g - 1)
         send_near_free(g)
         send_back(g - 1)
     send_near_late(GROUPS - 1)
+    send_sums_early()
     send_back(GROUPS - 1)
 
     mixture = jnp.zeros((RING * TOK, WIDTH), F32)
@@ -300,7 +357,11 @@
             if j:
                 returned[j].wait_recv()
         mixture = mixture + dot_nn(mix_hi[:, rows], back[rows, :]) + dot_nn(mix_lo[:, rows], back[rows, :])
-    z_out[...] = mixture.astype(BF16)
+    for copy in summed_early:
+        copy.wait_recv()
+    part = mixture[:, LATE:WIDTH] + early_sum[0].astype(F32) + early_sum[1].astype(F32) + early_sum[2].astype(F32)
+    z_out[:, 0:LATE] = mixture[:, 0:LATE].astype(BF16)
+    z_out[:, LATE:WIDTH] = part.astype(BF16)
     homes = []
     for du in FAR_FIRST:
         copy = remote(
@@ -309,13 +370,16 @@
         )
         copy.start()
         homes.append(copy)
-    total = mixture[0:TOK, :]
+    totals = [mixture[0:TOK, 0:LATE], part[0:TOK, :]]
     for du, copy in zip(FAR_FIRST, homes):
         copy.wait_recv()
-        total = total + z_in[du].astype(F32)
-    out[...] = total.astype(BF16)
-
-    for copy in gathers + routed[1:] + sum(sent + forwarded + far + near, []) + returned[1:] + homes:
+        totals[0] = totals[0] + z_in[du, :, 0:LATE].astype(F32)
+        totals[1] = totals[1] + z_in[du, :, LATE:WIDTH].astype(F32)
+    out[:, 0:LATE] = totals[0].astype(BF16)
+    out[:, LATE:WIDTH] = totals[1].astype(BF16)
+
+    early_copies = crossing + routed_early[1:] + returned_early[1:] + summed_early
+    for copy in gathers + routed[1:] + sum(sent + forwarded + far + near, []) + returned[1:] + homes + early_copies:
         copy.wait_send()
 
 
@@ -338,19 +402,27 @@
             pltpu.VMEM((RING, TOK, MSG), BF16),
             pltpu.VMEM((RING * TOK, MSG), BF16),
             pltpu.VMEM((SLOTS, WIDTH), BF16),
-            pltpu.VMEM((4, SLOTS, WIDTH), BF16),
+            pltpu.VMEM((SLOTS, WIDTH), BF16),
+            pltpu.VMEM((3, SLOTS, LATE), BF16),
             pltpu.VMEM((RING * TOK, SLOTS), BF16),
             pltpu.VMEM((RING * TOK, SLOTS), BF16),
             pltpu.VMEM((SLOTS, HID), BF16),
-            pltpu.VMEM((GROUPS, ROWS_G, WIDTH), BF16),
-            pltpu.VMEM((2, GROUPS, HALF_G, WIDTH), BF16),
-            pltpu.VMEM((2, GROUPS, HALF_G, WIDTH), F32),
-            pltpu.VMEM((2, GROUPS, ROWS_G, WIDTH), BF16),
-            pltpu.VMEM((2, GROUPS, ROWS_G, WIDTH), BF16),
+            pltpu.VMEM((GROUPS, ROWS_G, LATE), BF16),
+            pltpu.VMEM((2, GROUPS, HALF_G, LATE), BF16),
+            pltpu.VMEM((2, GROUPS, HALF_G, LATE), F32),
+            pltpu.VMEM((2, GROUPS, ROWS_G, LATE), BF16),
+            pltpu.VMEM((2, GROUPS, ROWS_G, LATE), BF16),
             pltpu.VMEM((SLOTS, WIDTH), BF16),
             pltpu.VMEM((SLOTS, WIDTH), BF16),
             pltpu.VMEM((RING * TOK, WIDTH), BF16),
             pltpu.VMEM((RING, TOK, WIDTH), BF16),
+            pltpu.VMEM((RING * TOK, 3 * EARLY), BF16),
+            pltpu.VMEM((SLOTS, 3 * EARLY), BF16),
+            pltpu.VMEM((SLOTS, 3 * EARLY), BF16),
+            pltpu.VMEM((SLOTS, 3 * EARLY), BF16),
+            pltpu.VMEM((SLOTS, 3 * EARLY), BF16),
+            pltpu.VMEM((RING * TOK, 3 * EARLY), BF16),
+            pltpu.VMEM((3, RING * TOK, EARLY), BF16),
             dma((10,)),
             dma((12,)),
             dma((7,)), dma((7,)),
@@ -361,6 +433,10 @@
             dma((2, GROUPS, 2)), dma((2, GROUPS, 2)),
             dma((16,)), dma((16,)),
             dma((7,)), dma((7,)),
+            dma((3,)), dma((3,)),
+            dma((16,)), dma((16,)),
+            dma((16,)), dma((16,)),
+            dma((3,)), dma((3,)),
         ],
         compiler_params=pltpu.CompilerParams(
             collective_id=0, has_side_effects=True, vmem_limit_bytes=62 * 1024 * 1024

time: 78.9 us -> 72.6 us (0.920)
  Pallas kernels: 77.3 us -> 71 us
    pallas_call x1, Pallas kernels: 77.3 us -> 71 us  [per_device(): pl.pallas_call(kernel, out_shape=jax.ShapeDtypeStruct((TOK, WIDTH), BF16)...]
where the time goes in v3:
time: 72.6 us; the launch traced here: 72.4 us
  Pallas kernels  71 us (98%)
  local copies, waits for them, and re-layouts  1.38 us (2%)
    pallas_call x1, Pallas kernels, per_device(): pl.pallas_call(kernel, out_shape=jax.ShapeDtypeStruct((TOK, WIDTH), BF16)...  71 us

profile of v3, /device:TPU:1, one launch (start us, length us, event | category | flops | bytes accessed | tf_op | source)
XLA Modules:
  0.0 72.4 jit_solution(17422619288604230884)
XLA Ops:
  0.0 71.0 %shard_map.64 = bf16[16,1024]{1,0:T(8,128)(2,1)} custom-call(bf16[16,1024]{1,0:T(8,128)(2,1)} %tok_hbm.1, s32[8,16]{1,0:T(8,128)} %bitcast.2, f32[8,16]{1,0:T(8,128)} %bitcast.3, bf16[1,192,4096]{2,1,0:T(8,128)(2,1)} %wg.1, bf16[1,192,4096]{2,1,0:T(8,128)(2,1)} %wu.1, bf16[1,192,4096]{2,1,0:T(8,128)(2,1)} %wd.1), custom_call_target="tpu_custom_call" | custom-call | tf_op jit(solution)/shard_map/pallas_call | solution.py:390
  71.0 1.4 %copy.8 = bf16[16,1024]{1,0:T(8,128)(2,1)} copy(bf16[16,1024]{1,0:T(8,128)(2,1)} %shard_map.64) | data formatting | bytes 65536

commit v4 on v3

--- a/solution.py
+++ b/solution.py
@@ -18,10 +18,13 @@
 ROWS_G = SLOTS // GROUPS
 HALF_G = ROWS_G // 2
 LAG = 2
-EARLY_AFTER = 3
+EARLY_AFTER = 1
 MSG = WIDTH + 128
-EARLY = 384
-LATE = WIDTH - EARLY
+EARLY_OUT = 384
+LATE_OUT = WIDTH - EARLY_OUT
+EARLY_BACK = 384
+SPLIT = 640
+PARTS = ((0, EARLY_BACK, WIDTH), (1, EARLY_BACK, SPLIT), (1, SPLIT, WIDTH))
 FAR_FIRST = (4, 3, 5, 2, 6, 1, 7)
 F32 = jnp.float32
 BF16 = jnp.bfloat16
@@ -46,9 +49,9 @@
 def kernel(
     tok_hbm, routes_hbm, probs_hbm, wg, wu, wd, out,
     routes, probs, wgv, wuv, wdv, pieces, snd, stg, outb, own, ring, mix_hi, mix_lo, hid,
-    a_out, a_in, b_late, b_out, b_in, y_out, back, z_out, z_in, early_tok, early_out, early, early_y, early_back, early_z, early_sum,
+    a_out, a_in, b_late, b_out, b_in, y_out, back, z_out, z_in, early_tok, early_out, early, early_y, early_back, early_z, early_in, early_send, early_sum,
     in_sem, w_sem, s1s, s1r, s2s, s2r, xss, xsr, fws, fwr, ras, rar, rbs, rbr, s3s, s3r, s4s, s4r,
-    ets, etr, ers, err, eys, eyr, ezs, ezr,
+    ets, etr, egs, egr, ers, err, eys, eyr, ehs, ehr, ezs, ezr,
 ):
     e = lax.axis_index("expert")
     x = lax.axis_index("pair")
@@ -137,7 +140,15 @@
             device_id=(expert, pair), device_id_type=pl.DeviceIdType.MESH,
         )
 
-    gathers = []
+    crossing = [None] * 3
+    for k in (2, 1, 3):
+        copy = remote(
+            stg.at[0:TOK, LATE_OUT:WIDTH], early_tok.at[0:TOK, (k - 1) * EARLY_OUT:k * EARLY_OUT],
+            ets.at[k - 1], etr.at[k - 1], e, (x + k) % 4,
+        )
+        copy.start()
+        crossing[k - 1] = copy
+    gathers, gathers_early = [], []
     for du in FAR_FIRST:
         copy = remote(
             snd.at[du], stg.at[du * TOK:(du + 1) * TOK, :], s1s.at[du - 1], s1r.at[du - 1],
@@ -147,16 +158,17 @@
         gathers.append(copy)
     slot = iota((SLOTS, 128), 0)
     spread = [ones_where(iota((SLOTS, 128), 1) == 32 * j + ((slot >> 4) << 1) + (slot & 1)) for j in range(2)]
+    for copy in crossing:
+        copy.wait_recv()
+    for du in FAR_FIRST:
+        copy = remote(
+            early_tok.at[0:TOK, :], early_tok.at[du * TOK:(du + 1) * TOK, :], egs.at[du - 1], egr.at[du - 1],
+            ((u + du) % RING) * su + v * sv + c, x,
+        )
+        copy.start()
+        gathers_early.append(copy)
     for copy in gathers:
         copy.wait_recv()
-
-    crossing = [None] * 3
-    for k in (2, 1, 3):
-        copy = remote(
-            stg.at[:, LATE:WIDTH], early_tok.at[:, (k - 1) * EARLY:k * EARLY], ets.at[k - 1], etr.at[k - 1], e, (x + k) % 4
-        )
-        copy.start()
-        crossing[k - 1] = copy
 
     source = stg[:, WIDTH:MSG]
     tok_du = iota((SLOTS, RING * TOK), 1) >> 4
@@ -172,7 +184,7 @@
         return slice(j * 16, (j + 1) * 16)
 
     def route_early():
-        for copy in crossing:
+        for copy in gathers_early:
             copy.wait_recv()
         early_out[...] = dot_nn(placing, early_tok[...]).astype(BF16)
         early[0:TOK, :] = early_out[0:TOK, :]
@@ -206,7 +218,7 @@
             if 2 * i + dc:
                 routed[2 * i + dc].wait_recv()
         for way, (k, target) in enumerate(((1, right), (3, left))):
-            copy = remote(own.at[rows, 0:LATE], ring.at[k - 1, rows, :], xss.at[way, i], xsr.at[way, i], e, target)
+            copy = remote(own.at[rows, 0:LATE_OUT], ring.at[k - 1, rows, :], xss.at[way, i], xsr.at[way, i], e, target)
             copy.start()
             sent[way][i] = copy
 
@@ -220,27 +232,28 @@
 
     def hidden(g):
         rows = slice(g * ROWS_G, (g + 1) * ROWS_G)
-        for i in range(g * PAIRS_G, (g + 1) * PAIRS_G):
+        pairs = range(g * PAIRS_G, (g + 1) * PAIRS_G)
+        weights = (wgv, wuv)
+        totals = [dot_nt(own[rows, :], w[0]) for w in weights]
+        for way, k in enumerate((1, 3)):
+            totals = [t + dot_nt(ring[k - 1, rows, :], w[k, :, 0:LATE_OUT]) for t, w in zip(totals, weights)]
+        for i in pairs:
+            for j in (2 * i, 2 * i + 1):
+                if j:
+                    routed_early[j].wait_recv()
+        for k in range(1, 4):
+            lanes = slice((k - 1) * EARLY_OUT, k * EARLY_OUT)
+            totals = [t + dot_nt(early[rows, lanes], w[k, :, LATE_OUT:WIDTH]) for t, w in zip(totals, weights)]
+        for i in pairs:
             for way in range(2):
                 forwarded[way][i].wait_recv()
-        for j in range(max(1, g * 2 * PAIRS_G), (g + 1) * 2 * PAIRS_G):
-            routed_early[j].wait_recv()
-
-        def product(weights):
-            total = dot_nt(own[rows, :], weights[0])
-            for k in range(1, 4):
-                total = total + dot_nt(ring[k - 1, rows, :], weights[k, :, 0:LATE])
-                total = total + dot_nt(early[rows, (k - 1) * EARLY:k * EARLY], weights[k, :, LATE:WIDTH])
-            return total
-
-        gate = product(wgv)
-        up = product(wuv)
+        gate, up = [t + dot_nt(ring[1, rows, :], w[2, :, 0:LATE_OUT]) for t, w in zip(totals, weights)]
         hid[rows, :] = (gate / (1.0 + jnp.exp(-gate)) * up).astype(BF16)
 
-    far = [None] * GROUPS
-    near = [None] * GROUPS
-
-    def down(g, k, lanes=slice(0, LATE)):
+    far = [None] * len(PARTS)
+    near = [None] * len(PARTS)
+
+    def down(g, k, lanes):
         return dot_nn(hid[g * ROWS_G:(g + 1) * ROWS_G, :], wdv[k, :, lanes])
 
     def source_of(j):
@@ -248,13 +261,13 @@
         u_s, v_s, su_s, sv_s = role(core)
         return u_s * su_s + ((v_s + RING - DV[j // 2]) % RING) * sv_s + core
 
-    returned = [None] * 16
+    returned = [None] * len(PARTS)
     returned_early = [None] * 16
 
     def send_back_early(g):
         rows = slice(g * ROWS_G, (g + 1) * ROWS_G)
         for k in range(1, 4):
-            early_y[rows, (k - 1) * EARLY:k * EARLY] = down(g, k, slice(LATE, WIDTH)).astype(BF16)
+            early_y[rows, (k - 1) * EARLY_BACK:k * EARLY_BACK] = down(g, k, slice(0, EARLY_BACK)).astype(BF16)
         if g == 0:
             early_back[0:TOK, :] = early_y[0:TOK, :]
         for j in range(max(1, g * 2 * PAIRS_G), (g + 1) * 2 * PAIRS_G):
@@ -265,62 +278,94 @@
     def halves(way):
         return slice(way * HALF_G, (way + 1) * HALF_G), slice((1 - way) * HALF_G, (2 - way) * HALF_G)
 
-    def send_far(g):
-        a_out[g] = down(g, 2).astype(BF16)
-        far[g] = []
+    def send_far(p):
+        g, first, last = PARTS[p]
+        lanes = slice(first, last)
+        a_out[g, :, lanes] = down(g, 2, lanes).astype(BF16)
+        far[p] = []
         for way, target in enumerate((right, left)):
-            copy = remote(a_out.at[g, halves(way)[0], :], a_in.at[way, g], ras.at[way, g], rar.at[way, g], e, target)
-            copy.start()
-            far[g].append(copy)
-
-    def send_near(way, g, rows, late):
-        target = left if way else right
+            copy = remote(
+                a_out.at[g, halves(way)[0], lanes], a_in.at[way, g, :, lanes], ras.at[way, p], rar.at[way, p], e, target
+            )
+            copy.start()
+            far[p].append(copy)
+
+    def send_near(way, p, rows, late):
+        g, first, last = PARTS[p]
         copy = remote(
-            b_out.at[way, g, rows, :], b_in.at[way, g, rows, :],
-            rbs.at[way, g, late], rbr.at[way, g, late], e, target,
+            b_out.at[way, g, rows, first:last], b_in.at[way, g, rows, first:last],
+            rbs.at[way, p, late], rbr.at[way, p, late], e, left if way else right,
         )
         copy.start()
-        near[g].append(copy)
-
-    def send_near_free(g):
-        near[g] = []
+        near[p].append(copy)
+
+    def send_near_free(p):
+        g, first, last = PARTS[p]
+        near[p] = []
         for way, k in enumerate((3, 1)):
             late, free = halves(way)
-            term = down(g, k)
-            b_late[way, g] = term[late, :]
-            b_out[way, g, free, :] = term[free, :].astype(BF16)
-            send_near(way, g, free, 0)
-
-    def send_near_late(g):
+            term = down(g, k, slice(first, last))
+            b_late[way, g, :, first:last] = term[late, :]
+            b_out[way, g, free, first:last] = term[free, :].astype(BF16)
+            send_near(way, p, free, 0)
+
+    def send_near_late(p):
+        g, first, last = PARTS[p]
+        lanes = slice(first, last)
         for way in range(2):
             late, _ = halves(way)
-            far[g][way].wait_recv()
-            b_out[way, g, late, :] = (b_late[way, g] + a_in[way, g].astype(F32)).astype(BF16)
-            send_near(way, g, late, 1)
-
-    def send_back(g):
+            far[p][way].wait_recv()
+            b_out[way, g, late, lanes] = (b_late[way, g, :, lanes] + a_in[way, g, :, lanes].astype(F32)).astype(BF16)
+            send_near(way, p, late, 1)
+
+    def send_back(p):
+        g, first, last = PARTS[p]
         rows = slice(g * ROWS_G, (g + 1) * ROWS_G)
-        term = down(g, 0)
-        y_out[rows, LATE:WIDTH] = down(g, 0, slice(LATE, WIDTH)).astype(BF16)
-        for copy in near[g]:
+        lanes = slice(first, last)
+        term = down(g, 0, lanes)
+        start = first
+        if first == EARLY_BACK:
+            start = 0
+            y_out[rows, 0:EARLY_BACK] = down(g, 0, slice(0, EARLY_BACK)).astype(BF16)
+        for copy in near[p]:
             copy.wait_recv()
-        y_out[rows, 0:LATE] = (term + b_in[0, g].astype(F32) + b_in[1, g].astype(F32)).astype(BF16)
+        y_out[rows, lanes] = (term + b_in[0, g, :, lanes].astype(F32) + b_in[1, g, :, lanes].astype(F32)).astype(BF16)
         if g == 0:
             back[0:TOK, :] = y_out[0:TOK, :]
+        returned[p] = []
         for j in range(max(1, g * 2 * PAIRS_G), (g + 1) * 2 * PAIRS_G):
-            copy = remote(y_out.at[rows_of(j), :], back.at[rows_of(j), :], s3s.at[j], s3r.at[j], source_of(j), x)
-            copy.start()
-            returned[j] = copy
-
+            copy = remote(
+                y_out.at[rows_of(j), start:last], back.at[rows_of(j), start:last], s3s.at[p, j], s3r.at[p, j], source_of(j), x
+            )
+            copy.start()
+            returned[p].append(copy)
+
+    def home_of(du):
+        return ((u + RING - du) % RING) * su + v * sv + c
+
+    homes_early, homes = [], []
     summed_early = [None] * 3
 
-    def send_sums_early():
+    def send_home_early():
         for copy in returned_early[1:]:
             copy.wait_recv()
-        early_z[...] = (dot_nn(mix_hi[...], early_back[...]) + dot_nn(mix_lo[...], early_back[...])).astype(BF16)
+        sums = dot_nn(mix_hi[...], early_back[...]) + dot_nn(mix_lo[...], early_back[...])
+        early_z[...] = sums.astype(BF16)
+        for du in FAR_FIRST:
+            copy = remote(early_z.at[du * TOK:(du + 1) * TOK, :], early_in.at[du], ehs.at[du - 1], ehr.at[du - 1], home_of(du), x)
+            copy.start()
+            homes_early.append(copy)
+        return sums[0:TOK, :]
+
+    def send_sums_early(sums):
+        for du, copy in zip(FAR_FIRST, homes_early):
+            copy.wait_recv()
+            sums = sums + early_in[du].astype(F32)
+        early_send[...] = sums.astype(BF16)
         for k in (2, 1, 3):
             copy = remote(
-                early_z.at[:, (k - 1) * EARLY:k * EARLY], early_sum.at[k - 1], ezs.at[k - 1], ezr.at[k - 1], e, (x + 4 - k) % 4
+                early_send.at[:, (k - 1) * EARLY_BACK:k * EARLY_BACK], early_sum.at[k - 1],
+                ezs.at[k - 1], ezr.at[k - 1], e, (x + 4 - k) % 4,
             )
             copy.start()
             summed_early[k - 1] = copy
@@ -337,49 +382,54 @@
     for i in range(RING - LAG, RING):
         forward_pair(i)
     send_far(0)
+    send_near_free(0)
     send_back_early(0)
-    send_near_free(0)
-    for g in range(1, GROUPS):
-        hidden(g)
-        send_far(g)
-        send_back_early(g)
-        send_near_late(g - 1)
-        send_near_free(g)
-        send_back(g - 1)
-    send_near_late(GROUPS - 1)
-    send_sums_early()
-    send_back(GROUPS - 1)
-
-    mixture = jnp.zeros((RING * TOK, WIDTH), F32)
-    for g in range(GROUPS):
-        rows = slice(g * ROWS_G, (g + 1) * ROWS_G)
-        for j in range(g * 2 * PAIRS_G, (g + 1) * 2 * PAIRS_G):
-            if j:
-                returned[j].wait_recv()
-        mixture = mixture + dot_nn(mix_hi[:, rows], back[rows, :]) + dot_nn(mix_lo[:, rows], back[rows, :])
-    for copy in summed_early:
+    hidden(1)
+    send_far(1)
+    send_far(2)
+    send_near_late(0)
+    send_back_early(1)
+    send_near_free(1)
+    send_near_free(2)
+    send_near_late(1)
+    send_near_late(2)
+    send_back(0)
+
+    send_back(1)
+    send_back(2)
+    sums_early = send_home_early()
+    halves_home = []
+    for h, (start, last) in enumerate(((0, SPLIT), (SPLIT, WIDTH))):
+        for copy in (returned[0] if h == 0 else []) + returned[1 + h]:
+            copy.wait_recv()
+        mixture = dot_nn(mix_hi[...], back[:, start:last]) + dot_nn(mix_lo[...], back[:, start:last])
+        z_out[:, start:last] = mixture.astype(BF16)
+        for du in FAR_FIRST:
+            copy = remote(
+                z_out.at[du * TOK:(du + 1) * TOK, start:last], z_in.at[du, :, start:last],
+                s4s.at[h, du - 1], s4r.at[h, du - 1], home_of(du), x,
+            )
+            copy.start()
+            homes.append(copy)
+        halves_home.append(mixture[0:TOK, :])
+    send_sums_early(sums_early)
+    for h, (start, last) in enumerate(((0, SPLIT), (SPLIT, WIDTH))):
+        total = halves_home[h]
+        for du, copy in zip(FAR_FIRST, homes[7 * h:]):
+            copy.wait_recv()
+            total = total + z_in[du, :, start:last].astype(F32)
+        if h == 0:
+            part = total[:, 0:EARLY_BACK]
+            out[:, EARLY_BACK:SPLIT] = total[:, EARLY_BACK:SPLIT].astype(BF16)
+        else:
+            out[:, SPLIT:WIDTH] = total.astype(BF16)
+    for k, copy in enumerate(summed_early):
         copy.wait_recv()
-    part = mixture[:, LATE:WIDTH] + early_sum[0].astype(F32) + early_sum[1].astype(F32) + early_sum[2].astype(F32)
-    z_out[:, 0:LATE] = mixture[:, 0:LATE].astype(BF16)
-    z_out[:, LATE:WIDTH] = part.astype(BF16)
-    homes = []
-    for du in FAR_FIRST:
-        copy = remote(
-            z_out.at[du * TOK:(du + 1) * TOK, :], z_in.at[du], s4s.at[du - 1], s4r.at[du - 1],
-            ((u + RING - du) % RING) * su + v * sv + c, x,
-        )
-        copy.start()
-        homes.append(copy)
-    totals = [mixture[0:TOK, 0:LATE], part[0:TOK, :]]
-    for du, copy in zip(FAR_FIRST, homes):
-        copy.wait_recv()
-        totals[0] = totals[0] + z_in[du, :, 0:LATE].astype(F32)
-        totals[1] = totals[1] + z_in[du, :, LATE:WIDTH].astype(F32)
-    out[:, 0:LATE] = totals[0].astype(BF16)
-    out[:, LATE:WIDTH] = totals[1].astype(BF16)
-
-    early_copies = crossing + routed_early[1:] + returned_early[1:] + summed_early
-    for copy in gathers + routed[1:] + sum(sent + forwarded + far + near, []) + returned[1:] + homes + early_copies:
+        part = part + early_sum[k].astype(F32)
+    out[:, 0:EARLY_BACK] = part.astype(BF16)
+
+    early_copies = crossing + gathers_early + routed_early[1:] + returned_early[1:] + homes_early + summed_early
+    for copy in gathers + routed[1:] + sum(sent + forwarded + far + near + returned, []) + homes + early_copies:
         copy.wait_send()
 
 
@@ -403,45 +453,52 @@
             pltpu.VMEM((RING * TOK, MSG), BF16),
             pltpu.VMEM((SLOTS, WIDTH), BF16),
             pltpu.VMEM((SLOTS, WIDTH), BF16),
-            pltpu.VMEM((3, SLOTS, LATE), BF16),
+            pltpu.VMEM((3, SLOTS, LATE_OUT), BF16),
             pltpu.VMEM((RING * TOK, SLOTS), BF16),
             pltpu.VMEM((RING * TOK, SLOTS), BF16),
             pltpu.VMEM((SLOTS, HID), BF16),
-            pltpu.VMEM((GROUPS, ROWS_G, LATE), BF16),
-            pltpu.VMEM((2, GROUPS, HALF_G, LATE), BF16),
-            pltpu.VMEM((2, GROUPS, HALF_G, LATE), F32),
-            pltpu.VMEM((2, GROUPS, ROWS_G, LATE), BF16),
-            pltpu.VMEM((2, GROUPS, ROWS_G, LATE), BF16),
+            pltpu.VMEM((GROUPS, ROWS_G, WIDTH), BF16),
+            pltpu.VMEM((2, GROUPS, HALF_G, WIDTH), BF16),
+            pltpu.VMEM((2, GROUPS, HALF_G, WIDTH), F32),
+            pltpu.VMEM((2, GROUPS, ROWS_G, WIDTH), BF16),
+            pltpu.VMEM((2, GROUPS, ROWS_G, WIDTH), BF16),
             pltpu.VMEM((SLOTS, WIDTH), BF16),
             pltpu.VMEM((SLOTS, WIDTH), BF16),
             pltpu.VMEM((RING * TOK, WIDTH), BF16),
             pltpu.VMEM((RING, TOK, WIDTH), BF16),
-            pltpu.VMEM((RING * TOK, 3 * EARLY), BF16),
-            pltpu.VMEM((SLOTS, 3 * EARLY), BF16),
-            pltpu.VMEM((SLOTS, 3 * EARLY), BF16),
-            pltpu.VMEM((SLOTS, 3 * EARLY), BF16),
-            pltpu.VMEM((SLOTS, 3 * EARLY), BF16),
-            pltpu.VMEM((RING * TOK, 3 * EARLY), BF16),
-            pltpu.VMEM((3, RING * TOK, EARLY), BF16),
+            pltpu.VMEM((RING * TOK, 3 * EARLY_OUT), BF16),
+            pltpu.VMEM((SLOTS, 3 * EARLY_OUT), BF16),
+            pltpu.VMEM((SLOTS, 3 * EARLY_OUT), BF16),
+            pltpu.VMEM((SLOTS, 3 * EARLY_BACK), BF16),
+            pltpu.VMEM((SLOTS, 3 * EARLY_BACK), BF16),
+            pltpu.VMEM((RING * TOK, 3 * EARLY_BACK), BF16),
+            pltpu.VMEM((RING, TOK, 3 * EARLY_BACK), BF16),
+            pltpu.VMEM((TOK, 3 * EARLY_BACK), BF16),
+            pltpu.VMEM((3, TOK, EARLY_BACK), BF16),
             dma((10,)),
             dma((12,)),
             dma((7,)), dma((7,)),
             dma((16,)), dma((16,)),
             dma((2, RING)), dma((2, RING)),
             dma((2, RING)), dma((2, RING)),
-            dma((2, GROUPS)), dma((2, GROUPS)),
-            dma((2, GROUPS, 2)), dma((2, GROUPS, 2)),
+            dma((2, len(PARTS))), dma((2, len(PARTS))),
+            dma((2, len(PARTS), 2)), dma((2, len(PARTS), 2)),
+            dma((len(PARTS), 16)), dma((len(PARTS), 16)),
+            dma((2, 7)), dma((2, 7)),
+            dma((3,)), dma((3,)),
+            dma((7,)), dma((7,)),
+            dma((16,)), dma((16,)),
             dma((16,)), dma((16,)),
             dma((7,)), dma((7,)),
             dma((3,)), dma((3,)),
-            dma((16,)), dma((16,)),
-            dma((16,)), dma((16,)),
-            dma((3,)), dma((3,)),
         ],
         compiler_params=pltpu.CompilerParams(
-            collective_id=0, has_side_effects=True, vmem_limit_bytes=62 * 1024 * 1024
+            collective_id=0, has_side_effects=True, vmem_limit_bytes=40 * 1024 * 1024
         ),
-    )(tokens, routes.T, router_probs.T, w_gate, w_up, w_down)
+    )(*(
+        pltpu.with_memory_space_constraint(a, pltpu.HBM)
+        for a in (tokens, routes.T, router_probs.T, w_gate, w_up, w_down)
+    ))
 
 
 def solution(mesh):

time: 72.6 us -> 68.6 us (0.945)
  Pallas kernels: 71 us -> 67.2 us
  local copies, waits for them, and re-layouts: 1.38 us -> 0.62 us
    pallas_call x1, Pallas kernels: 71 us -> 67.2 us  [per_device(): pl.pallas_call(kernel, out_shape=jax.ShapeDtypeStruct((TOK, WIDTH), BF16)...]
    unnamed x1, local copies, waits for them, and re-layouts: 1.38 us -> 0.62 us
where the time goes in v4:
time: 68.6 us; the launch traced here: 67.8 us
  Pallas kernels  67.2 us (98%)
    pallas_call x1, Pallas kernels, per_device(): pl.pallas_call(kernel, out_shape=jax.ShapeDtypeStruct((TOK, WIDTH), BF16)...  67.2 us

profile of v4, /device:TPU:1, one launch (start us, length us, event | category | flops | bytes accessed | tf_op | source)
XLA Modules:
  0.0 67.8 jit_solution(14971764847069387709)
XLA Ops:
  0.0 67.2 %shard_map.64 = bf16[16,1024]{1,0:T(8,128)(2,1)S(1)} custom-call(bf16[16,1024]{1,0:T(8,128)(2,1)} %tok_hbm.1, s32[8,16]{1,0:T(8,128)} %bitcast.2, f32[8,16]{1,0:T(8,128)} %bitcast.3, bf16[1,192,4096]{2,1,0:T(8,128)(2,1)} %wg.1, bf16[1,192,4096]{2,1,0:T(8,128)(2,1)} %wu.1, bf16[1,192,4096]{2,1,0:T(8,128)(2,1)} %wd.1), custom_call_target="tpu_custom_call" | custom-call | tf_op jit(solution)/shard_map/pallas_call | solution.py:440
  67.2 0.6 copy.8

commit v5 on v4

--- a/solution.py
+++ b/solution.py
@@ -17,13 +17,13 @@
 PAIRS_G = RING // GROUPS
 ROWS_G = SLOTS // GROUPS
 HALF_G = ROWS_G // 2
-LAG = 2
+LAG = 3
 EARLY_AFTER = 1
 MSG = WIDTH + 128
 EARLY_OUT = 384
 LATE_OUT = WIDTH - EARLY_OUT
 EARLY_BACK = 384
-SPLIT = 640
+SPLIT = 512
 PARTS = ((0, EARLY_BACK, WIDTH), (1, EARLY_BACK, SPLIT), (1, SPLIT, WIDTH))
 FAR_FIRST = (4, 3, 5, 2, 6, 1, 7)
 F32 = jnp.float32
@@ -48,9 +48,9 @@
 
 def kernel(
     tok_hbm, routes_hbm, probs_hbm, wg, wu, wd, out,
-    routes, probs, wgv, wuv, wdv, pieces, snd, stg, outb, own, ring, mix_hi, mix_lo, hid,
+    routes, probs, wgv, wuv, wdv, pick, snd, stg, outb, own, ring, mix_hi, mix_lo, hid,
     a_out, a_in, b_late, b_out, b_in, y_out, back, z_out, z_in, early_tok, early_out, early, early_y, early_back, early_z, early_in, early_send, early_sum,
-    in_sem, w_sem, s1s, s1r, s2s, s2r, xss, xsr, fws, fwr, ras, rar, rbs, rbr, s3s, s3r, s4s, s4r,
+    in_sem, w_sem, s1s, s1r, sbs, sbr, s2s, s2r, xss, xsr, fws, fwr, ras, rar, rbs, rbr, s3s, s3r, s4s, s4r,
     ets, etr, egs, egr, ers, err, eys, eyr, ehs, ehr, ezs, ezr,
 ):
     e = lax.axis_index("expert")
@@ -82,12 +82,10 @@
         greet(e, (x + k) % 4)
 
     inputs = [
-        pltpu.make_async_copy(routes_hbm, routes, in_sem.at[8]),
-        pltpu.make_async_copy(probs_hbm, probs, in_sem.at[9]),
+        pltpu.make_async_copy(routes_hbm, routes, in_sem.at[1]),
+        pltpu.make_async_copy(probs_hbm, probs, in_sem.at[2]),
         pltpu.make_async_copy(tok_hbm, stg.at[0:TOK, 0:WIDTH], in_sem.at[0]),
     ]
-    for du in FAR_FIRST:
-        inputs.append(pltpu.make_async_copy(tok_hbm, snd.at[du, :, 0:WIDTH], in_sem.at[du]))
     for copy in inputs:
         copy.start()
 
@@ -98,6 +96,42 @@
             copy = pltpu.make_async_copy(src.at[0, :, quarter], dst.at[k], w_sem.at[3 * k + j])
             copy.start()
             loads.append(copy)
+
+    lane = iota((RING * 128, 1), 0)
+    pair = (lane >> 2) & 7
+    offset = jnp.where((pair & 1) == 1, (pair + 1) >> 1, (8 - (pair >> 1)) & 7)
+    owner = ((u + (lane >> 7)) & 7) * su + ((v + offset) & 7) * sv + ((c + (lane >> 1)) & 1)
+    column = ((lane >> 5) & 3) * 2 * EXPERTS + (lane & 1) * EXPERTS + owner
+    pick[...] = ones_where(iota((RING * 128, 4 * EXPERTS), 1) == column)
+
+    inputs[2].wait()
+    pl.semaphore_wait(barrier, 32)
+
+    def remote(src, dst, send, recv, expert, pair):
+        return pltpu.make_async_remote_copy(
+            src_ref=src, dst_ref=dst, send_sem=send, recv_sem=recv,
+            device_id=(expert, pair), device_id_type=pl.DeviceIdType.MESH,
+        )
+
+    crossing = [None] * 3
+    for k in (2, 1, 3):
+        copy = remote(
+            stg.at[0:TOK, LATE_OUT:WIDTH], early_tok.at[0:TOK, (k - 1) * EARLY_OUT:k * EARLY_OUT],
+            ets.at[k - 1], etr.at[k - 1], e, (x + k) % 4,
+        )
+        copy.start()
+        crossing[k - 1] = copy
+
+    def peer_of(du):
+        return ((u + du) % RING) * su + v * sv + c
+
+    gathers, gathers_early = [], []
+    for du in FAR_FIRST:
+        copy = remote(
+            stg.at[0:TOK, 0:WIDTH], stg.at[du * TOK:(du + 1) * TOK, 0:WIDTH], s1s.at[du - 1], s1r.at[du - 1], peer_of(du), x
+        )
+        copy.start()
+        gathers.append(copy)
 
     inputs[0].wait()
     inputs[1].wait()
@@ -112,50 +146,19 @@
     row, col = iota((TOK, TOK), 0), iota((TOK, TOK), 1)
     second = dot_nn(named, ones_where(row < col)) > 0.5
     same_token = ones_where(row == col)
-    for r in range(2):
-        part = jnp.where(second, mix, 0.0) if r else jnp.where(second, 0.0, mix)
-        high = part.astype(BF16)
-        low = (part - high.astype(F32)).astype(BF16)
-        for j, piece in enumerate((high, low)):
-            start = (2 * j + r) * EXPERTS
-            pieces[:, start:start + EXPERTS] = dot_nt(same_token, piece).astype(BF16)
-    lane = iota((RING * 128, 1), 0)
-    pair = (lane >> 2) & 7
-    offset = jnp.where((pair & 1) == 1, (pair + 1) >> 1, (8 - (pair >> 1)) & 7)
-    owner = ((u + (lane >> 7)) & 7) * su + ((v + offset) & 7) * sv + ((c + (lane >> 1)) & 1)
-    column = ((lane >> 5) & 3) * 2 * EXPERTS + (lane & 1) * EXPERTS + owner
-    pick = ones_where(iota((RING * 128, 4 * EXPERTS), 1) == column)
-    blocks = dot_nt(pieces[...], pick).astype(BF16)
+    parts = [jnp.where(second, 0.0, mix), jnp.where(second, mix, 0.0)]
+    pieces = [part.astype(BF16) for part in parts]
+    pieces += [(part - high.astype(F32)).astype(BF16) for part, high in zip(parts, pieces)]
+    blocks = dot_nt(dot_nt(same_token, jnp.concatenate(pieces, axis=0)).astype(BF16), pick[...]).astype(BF16)
     stg[0:TOK, WIDTH:MSG] = blocks[:, 0:128]
-    for du in range(1, RING):
-        snd[du, :, WIDTH:MSG] = blocks[:, du * 128:(du + 1) * 128]
-    for copy in inputs[2:]:
-        copy.wait()
-
-    pl.semaphore_wait(barrier, 32)
-
-    def remote(src, dst, send, recv, expert, pair):
-        return pltpu.make_async_remote_copy(
-            src_ref=src, dst_ref=dst, send_sem=send, recv_sem=recv,
-            device_id=(expert, pair), device_id_type=pl.DeviceIdType.MESH,
-        )
-
-    crossing = [None] * 3
-    for k in (2, 1, 3):
+    for du in FAR_FIRST:
+        snd[du] = blocks[:, du * 128:(du + 1) * 128]
         copy = remote(
-            stg.at[0:TOK, LATE_OUT:WIDTH], early_tok.at[0:TOK, (k - 1) * EARLY_OUT:k * EARLY_OUT],
-            ets.at[k - 1], etr.at[k - 1], e, (x + k) % 4,
-        )
-        copy.start()
-        crossing[k - 1] = copy
-    gathers, gathers_early = [], []
-    for du in FAR_FIRST:
-        copy = remote(
-            snd.at[du], stg.at[du * TOK:(du + 1) * TOK, :], s1s.at[du - 1], s1r.at[du - 1],
-            ((u + du) % RING) * su + v * sv + c, x,
+            snd.at[du], stg.at[du * TOK:(du + 1) * TOK, WIDTH:MSG], sbs.at[du - 1], sbr.at[du - 1], peer_of(du), x
         )
         copy.start()
         gathers.append(copy)
+
     slot = iota((SLOTS, 128), 0)
     spread = [ones_where(iota((SLOTS, 128), 1) == 32 * j + ((slot >> 4) << 1) + (slot & 1)) for j in range(2)]
     for copy in crossing:
@@ -163,7 +166,7 @@
     for du in FAR_FIRST:
         copy = remote(
             early_tok.at[0:TOK, :], early_tok.at[du * TOK:(du + 1) * TOK, :], egs.at[du - 1], egr.at[du - 1],
-            ((u + du) % RING) * su + v * sv + c, x,
+            peer_of(du), x,
         )
         copy.start()
         gathers_early.append(copy)
@@ -448,8 +451,8 @@
             pltpu.VMEM((4, HID, WIDTH), BF16),
             pltpu.VMEM((4, HID, WIDTH), BF16),
             pltpu.VMEM((4, HID, WIDTH), BF16),
-            pltpu.VMEM((TOK, 4 * EXPERTS), BF16),
-            pltpu.VMEM((RING, TOK, MSG), BF16),
+            pltpu.VMEM((RING * 128, 4 * EXPERTS), BF16),
+            pltpu.VMEM((RING, TOK, 128), BF16),
             pltpu.VMEM((RING * TOK, MSG), BF16),
             pltpu.VMEM((SLOTS, WIDTH), BF16),
             pltpu.VMEM((SLOTS, WIDTH), BF16),
@@ -475,8 +478,9 @@
             pltpu.VMEM((RING, TOK, 3 * EARLY_BACK), BF16),
             pltpu.VMEM((TOK, 3 * EARLY_BACK), BF16),
             pltpu.VMEM((3, TOK, EARLY_BACK), BF16),
-            dma((10,)),
+            dma((3,)),
             dma((12,)),
+            dma((7,)), dma((7,)),
             dma((7,)), dma((7,)),
             dma((16,)), dma((16,)),
             dma((2, RING)), dma((2, RING)),

time: 68.6 us -> 67.9 us (0.990)
  Pallas kernels: 67.2 us -> 66.3 us
    pallas_call x1, Pallas kernels: 67.2 us -> 66.3 us  [per_device(): pl.pallas_call(kernel, out_shape=jax.ShapeDtypeStruct((TOK, WIDTH), BF16)...]
where the time goes in v5:
time: 67.9 us; the launch traced here: 67 us
  Pallas kernels  66.3 us (98%)
    pallas_call x1, Pallas kernels, per_device(): pl.pallas_call(kernel, out_shape=jax.ShapeDtypeStruct((TOK, WIDTH), BF16)...  66.3 us

profile of v5, /device:TPU:1, one launch (start us, length us, event | category | flops | bytes accessed | tf_op | source)
XLA Modules:
  0.0 67.0 jit_solution(14498390194413789754)
XLA Ops:
  0.0 66.3 %shard_map.64 = bf16[16,1024]{1,0:T(8,128)(2,1)S(1)} custom-call(bf16[16,1024]{1,0:T(8,128)(2,1)} %tok_hbm.1, s32[8,16]{1,0:T(8,128)} %bitcast.2, f32[8,16]{1,0:T(8,128)} %bitcast.3, bf16[1,192,4096]{2,1,0:T(8,128)(2,1)} %wg.1, bf16[1,192,4096]{2,1,0:T(8,128)(2,1)} %wu.1, bf16[1,192,4096]{2,1,0:T(8,128)(2,1)} %wd.1), custom_call_target="tpu_custom_call" | custom-call | tf_op jit(solution)/shard_map/pallas_call | solution.py:443
  66.4 0.6 copy.8
